TPU v7x, 32 devices: a whole 2x2x4 slice. The times are simulated.
32 devices in a mesh: req: 16 (over z, y, x), tp: 2 (over core).
Axes of the slice: x: 2, y: 2, z: 4, core: 2. Of those that a mesh axis runs over, the one named last changes fastest.
Arguments:
- hidden_in: bfloat16 [4, 64, 3072], P(None, 'req', 'tp'), may hold values from -6 to 6
- norm_gain: float32 [3072], replicated, may hold values from 0.1 to 1.9
- w_query: bfloat16 [3072, 2048], P(None, 'tp'), may hold values from -1 to 1
- w_key: bfloat16 [3072, 1024], P(None, 'tp'), may hold values from -1 to 1
- w_value: bfloat16 [3072, 1024], P(None, 'tp'), may hold values from -0.109375 to 0.109375
- w_out: bfloat16 [2048, 3072], P('tp'), may hold values from -0.125 to 0.125
- prompt_keys: bfloat16 [16, 512, 1024], P('req', None, 'tp'), may hold values from -100 to 100
- prompt_values: bfloat16 [16, 512, 1024], P('req', None, 'tp'), may hold values from -8 to 8
- gen_keys: bfloat16 [64, 64, 1024], P('req', None, 'tp'), may hold values from -9 to 9
- gen_values: bfloat16 [64, 64, 1024], P('req', None, 'tp'), may hold values from -8 to 8
- lengths: int32 [8], replicated, may hold values from 768 to 1024, as said below
- parents: int32 [4, 64], replicated, may hold values from 0 to 7
Outputs:
- attended: bfloat16 [4, 64, 3072], P(None, 'req', 'tp')
Inputs may be any that keep to these rules, and one draw needn't show every extreme that they name: `lengths`: one request has a prompt of exactly 1024 tokens.
All inputs are finite; a program needn't handle non-finite values.
Results may differ from a plain program's by a relative error of at most 0.028.
Values may be sent and summed in bfloat16 or wider, within the bound.
No kernel may reach another device: no remote copies, remote signals or barrier semaphores. Data moves between devices by JAX's collectives and lax.ppermute only.
A program may use at most 64 MiB of HBM per device.

v0:
```python
import jax
import jax.numpy as jnp
from jax import lax
from jax.sharding import PartitionSpec as P

HD = 128


norm_eps = 1e-05
masked_score = -1e30
rope_base = 500000.0


def from_partner(value, axis, distance):
    mask = 2**distance
    pairs = [(source, source ^ mask) for source in range(lax.axis_size(axis))]
    return lax.ppermute(value, axis, pairs)


def rotate(vectors, positions):
    half_dim = vectors.shape[-1] // 2
    inverse = rope_base ** (-jnp.arange(half_dim, dtype=jnp.float32) / half_dim)
    angles = positions.astype(jnp.float32)[:, None, None] * inverse
    cosine = jnp.cos(angles)
    sine_part = jnp.sin(angles)
    first = vectors[..., :half_dim]
    second = vectors[..., half_dim:]
    return jnp.concatenate(
        [first * cosine - second * sine_part, second * cosine + first * sine_part], axis=-1
    )


def prompt_partial(queries, prompt_k, prompt_v, usable):
    scaling = queries.shape[-1] ** (-0.5)
    scores = (
        jnp.einsum("bkgd,pkd->bkgp", queries, prompt_k, preferred_element_type=jnp.float32)
        * scaling
    )
    scores = jnp.where(usable, scores, masked_score)
    highest = jnp.max(scores, axis=-1)
    weights = jnp.where(usable, jnp.exp(scores - highest[..., None]), 0.0)
    totals = jnp.sum(weights, axis=-1)
    weighted = jnp.einsum(
        "bkgp,pkd->bkgd", weights.astype(jnp.bfloat16), prompt_v, preferred_element_type=jnp.float32
    )
    return (highest, totals, weighted)


def history_partial(queries, hist_k, hist_v):
    scaling = queries.shape[-1] ** (-0.5)
    scores = (
        jnp.einsum("bkgd,btkd->bkgt", queries, hist_k, preferred_element_type=jnp.float32) * scaling
    )
    highest = jnp.max(scores, axis=-1)
    weights = jnp.exp(scores - highest[..., None])
    totals = jnp.sum(weights, axis=-1)
    weighted = jnp.einsum(
        "bkgt,btkd->bkgd", weights.astype(jnp.bfloat16), hist_v, preferred_element_type=jnp.float32
    )
    return (highest, totals, weighted)


def combine(first_part, second_part):
    joined = jnp.maximum(first_part[0], second_part[0])
    first_scale = jnp.exp(first_part[0] - joined)
    second_scale = jnp.exp(second_part[0] - joined)
    totals = first_part[1] * first_scale + second_part[1] * second_scale
    weighted = first_part[2] * first_scale[..., None] + second_part[2] * second_scale[..., None]
    return (joined, totals, weighted)


def in_order(mine, partner, parity):
    return jnp.where(
        parity == 0,
        jnp.concatenate([mine, partner], axis=0),
        jnp.concatenate([partner, mine], axis=0),
    )


def finish(step_queries, hist_k, hist_v, prompt_part, step, own_beams):
    lower = step * own_beams
    piece = (
        prompt_part[0][lower : lower + own_beams],
        prompt_part[1][lower : lower + own_beams],
        prompt_part[2][lower : lower + own_beams],
    )
    merged = combine(piece, history_partial(step_queries, hist_k, hist_v))
    context = merged[2] / merged[1][..., None]
    return context.reshape(own_beams, -1).astype(jnp.bfloat16)


def body(
    hidden_in,
    norm_gain,
    w_query,
    w_key,
    w_value,
    w_out,
    prompt_keys,
    prompt_values,
    gen_keys,
    gen_values,
    lengths,
    parents,
):
    steps_count, own_beams, _ = hidden_in.shape
    head_dim = HD
    kv_local = w_key.shape[1] // head_dim
    q_group = w_query.shape[1] // w_key.shape[1]
    half_len = prompt_keys.shape[1]
    history_start = gen_keys.shape[1]
    device = lax.axis_index("req")
    request = device // 2
    parity = device % 2
    length = lax.dynamic_index_in_dim(lengths, request, 0, keepdims=False)
    whole = lax.all_gather(hidden_in, "tp", axis=2, tiled=True)
    inputs = whole.astype(jnp.float32)
    inverse = lax.rsqrt(jnp.mean(inputs * inputs, axis=-1, keepdims=True) + norm_eps)
    total_rows = steps_count * own_beams
    normed = (inputs * inverse * norm_gain).astype(jnp.bfloat16).reshape(total_rows, -1)
    positions = jnp.repeat(
        length + history_start + jnp.arange(steps_count, dtype=jnp.int32), own_beams
    )
    queries = jnp.dot(normed, w_query, preferred_element_type=jnp.float32).reshape(
        total_rows, kv_local * q_group, head_dim
    )
    queries = (
        rotate(queries, positions)
        .astype(jnp.bfloat16)
        .reshape(total_rows, kv_local, q_group, head_dim)
    )
    new_keys = jnp.dot(normed, w_key, preferred_element_type=jnp.float32).reshape(
        total_rows, kv_local, head_dim
    )
    new_keys = rotate(new_keys, positions).astype(jnp.bfloat16)
    new_values = (
        jnp.dot(normed, w_value, preferred_element_type=jnp.float32)
        .astype(jnp.bfloat16)
        .reshape(total_rows, kv_local, head_dim)
    )
    own_k = prompt_keys.reshape(half_len, kv_local, head_dim)
    own_v = prompt_values.reshape(half_len, kv_local, head_dim)
    usable = parity * half_len + jnp.arange(half_len, dtype=jnp.int32) < length
    partner_queries = from_partner(queries, "req", 0)
    both = prompt_partial(jnp.concatenate([queries, partner_queries], axis=0), own_k, own_v, usable)
    returned = from_partner(
        (both[0][total_rows:], both[1][total_rows:], both[2][total_rows:]), "req", 0
    )
    prompt_part = combine(
        (both[0][:total_rows], both[1][:total_rows], both[2][:total_rows]), returned
    )
    hist_k = gen_keys.reshape(own_beams, history_start, kv_local, head_dim)
    hist_v = gen_values.reshape(own_beams, history_start, kv_local, head_dim)
    step_keys = new_keys.reshape(steps_count, own_beams, kv_local, head_dim)
    step_values = new_values.reshape(steps_count, own_beams, kv_local, head_dim)
    step_queries = queries.reshape(steps_count, own_beams, kv_local, q_group, head_dim)
    contexts = []
    for step in range(steps_count):
        other_k, other_v = from_partner((hist_k, hist_v), "req", 0)
        chosen = lax.dynamic_slice_in_dim(parents[step], device * own_beams, own_beams)
        hist_k = jnp.concatenate(
            [jnp.take(in_order(hist_k, other_k, parity), chosen, axis=0), step_keys[step][:, None]],
            axis=1,
        )
        hist_v = jnp.concatenate(
            [
                jnp.take(in_order(hist_v, other_v, parity), chosen, axis=0),
                step_values[step][:, None],
            ],
            axis=1,
        )
        contexts.append(finish(step_queries[step], hist_k, hist_v, prompt_part, step, own_beams))
    context_all = jnp.concatenate(contexts, axis=0)
    reduced = lax.psum_scatter(
        lax.dot_general(
            w_out, context_all, (((0,), (1,)), ((), ())), preferred_element_type=jnp.float32
        ).astype(jnp.bfloat16),
        "tp",
        scatter_dimension=0,
        tiled=True,
    ).astype(jnp.float32)
    return reduced.T.reshape(steps_count, own_beams, -1).astype(jnp.bfloat16)


def solution(mesh):
    in_specs = (
        P(None, "req", "tp"),
        P(),
        P(None, "tp"),
        P(None, "tp"),
        P(None, "tp"),
        P("tp", None),
        P("req", None, "tp"),
        P("req", None, "tp"),
        P("req", None, "tp"),
        P("req", None, "tp"),
        P(),
        P(),
    )
    out_specs = P(None, "req", "tp")
    return jax.shard_map(body, mesh=mesh, in_specs=in_specs, out_specs=out_specs, check_vma=False)
```

profile of v0, /device:TPU:0, one launch (start us, length us, event | category | flops | bytes accessed | tf_op | source)
XLA Modules:
  0.0 172.8 jit_solution(7363652386143385560)
XLA Ops:
  8.4 2.9 %collective-permute-start.3 = (bf16[4,64,4,128]{3,1,2,0:T(8,128)(2,1)}, bf16[4,64,4,128]{3,1,2,0:T(8,128)(2,1)}, u32[]{:S(2)}, u32[]{:S(2)}) collective-permute-start(bf16[4,64,4,128]{3,1,2,0:T(8,128)(2,1)} %copy_bitcast_fusion.1), channel_id=1, source_target_pairs={{0,2},{2,0},{4,6},{6,4},{8,10},{10,8},{12,14},{14,12},{16,18},{18,... | collective-permute-start | bytes 786440 | tf_op jit(solution)/shard_map/ppermute | solution.py:17
  12.5 2.3 %all_gather.3 = bf16[4,4,3072]{2,1,0:T(4,128)(2,1)S(1)} all-gather(bf16[4,4,1536]{2,1,0:T(4,128)(2,1)} %param.20), channel_id=1, replica_groups=mesh['req'=16,'tp'=2] {'tp'}, dimensions={2}, use_global_device_ids=true | all-gather | bytes 147456 | tf_op jit(solution)/shard_map/all_gather | solution.py:116
  18.1 8.6 %copy.224 = bf16[1024,3072]{1,0:T(8,128)(2,1)} copy(bf16[1024,3072]{0,1:T(8,128)(2,1)} %bitcast.75) | data formatting | bytes 12582912 | tf_op jit(solution)/shard_map/dot_general | solution.py:124
  26.8 4.5 %fusion.117 = f32[16,8,128]{2,0,1:T(8,128)S(1)} fusion(bf16[16,3072,1]{1,0,2:T(8,128)(2,1)S(1)} %reshape.275, bf16[8,128,3072]{2,1,0:T(8,128)(2,1)} %bitcast.73), kind=kOutput, calls=%fused_computation.216 | convolution fusion | flops 100663296 | bytes 6455296 | tf_op jit(solution)/shard_map/dot_general | solution.py:124
  37.8 4.6 %copy.229 = bf16[512,3072]{1,0:T(8,128)(2,1)} copy(bf16[512,3072]{0,1:T(8,128)(2,1)} %bitcast.76) | data formatting | bytes 6291456 | tf_op jit(solution)/shard_map/dot_general | solution.py:132
  42.4 2.8 %fusion.118 = f32[16,4,128]{2,0,1:T(8,128)S(1)} fusion(bf16[16,3072,1]{1,0,2:T(8,128)(2,1)S(1)} %reshape.275, bf16[4,128,3072]{2,1,0:T(8,128)(2,1)} %bitcast.74), kind=kOutput, calls=%fused_computation.217 | convolution fusion | flops 50331648 | bytes 3276800 | tf_op jit(solution)/shard_map/dot_general | solution.py:132
  63.5 2.0 %collective-permute-start.1 = (f32[16,4,2]{1,0,2:T(8,128)S(1)}, f32[16,4,2]{1,0,2:T(8,128)}, u32[]{:S(2)}, u32[]{:S(2)}) collective-permute-start(f32[16,4,2]{1,0,2:T(8,128)S(1)} %copy.231), channel_id=1, source_target_pairs={{0,2},{2,0},{4,6},{6,4},{8,10},{10,8},{12,14},{14,12},{16,18},{18,... | collective-permute-start | bytes 1544 | tf_op jit(solution)/shard_map/ppermute | solution.py:17
  73.0 2.1 %maximum_select_fusion.6 = bf16[8,64,4,128]{3,1,2,0:T(8,128)(2,1)} fusion(bf16[4,64,4,128]{3,1,2,0:T(8,128)(2,1)} %collective-permute-done.3, bf16[4,64,4,128]{3,1,2,0:T(8,128)(2,1)} %copy_bitcast_fusion.1, pred[]{:T(512)S(6)} %eq.4), kind=kLoop, calls=%fused_computation.25 | loop fusion | flops 786432 | bytes 1048577 | tf_op jit(solution)/shard_map/jit(_where)/select_n | solution.py:73
  75.1 2.5 %gather_fusion = bf16[4,64,4,128]{3,1,2,0:T(8,128)(2,1)} fusion(bf16[8,64,4,128]{3,1,2,0:T(8,128)(2,1)} %maximum_select_fusion.6, s32[1024]{0:T(1024)} %pad_clamp_fusion.3), kind=kCustom, calls=%fused_computation.clone | custom fusion | bytes 524304 | tf_op jit(solution)/shard_map/jit(_take)/gather | solution.py:162
  79.5 2.5 %gather_fusion.1 = bf16[4,64,4,128]{3,1,2,0:T(8,128)(2,1)} fusion(bf16[8,64,4,128]{3,1,2,0:T(8,128)(2,1)} %maximum_select_fusion.7, s32[1024]{0:T(1024)} %pad_clamp_fusion.3), kind=kCustom, calls=%fused_computation.4.clone | custom fusion | bytes 524304 | tf_op jit(solution)/shard_map/jit(_take)/gather | solution.py:167
  89.6 5.0 %collective-permute-done.6 = bf16[4,65,4,128]{3,1,2,0:T(8,128)(2,1)} collective-permute-done((bf16[4,65,4,128]{3,1,2,0:T(8,128)(2,1)}, bf16[4,65,4,128]{3,1,2,0:T(8,128)(2,1)}, u32[]{:S(2)}, u32[]{:S(2)}) %collective-permute-start.6) | collective-permute-done | bytes 266272 | tf_op jit(solution)/shard_map/ppermute | solution.py:17
  94.6 2.2 %maximum_select_fusion = bf16[8,65,4,128]{3,1,2,0:T(8,128)(2,1)} fusion(bf16[4,65,4,128]{3,1,2,0:T(8,128)(2,1)} %collective-permute-done.6, bf16[4,1,4,128]{3,1,2,0:T(2,128)(2,1)S(1)} %copy-done.11, bf16[4,64,4,128]{3,1,2,0:T(8,128)(2,1)} %copy-done.3, pred[]{:T(512)S(6)} %eq.4), kind=kLoop, calls=%fused_computation.19 | loop fusion | flops 3461120 | bytes 1064961 | tf_op jit(solution)/shard_map/jit(_where)/select_n | solution.py:73
  96.8 2.5 %gather_fusion.2 = bf16[4,65,4,128]{3,1,2,0:T(8,128)(2,1)} fusion(bf16[8,65,4,128]{3,1,2,0:T(8,128)(2,1)} %maximum_select_fusion, s32[1024]{0:T(1024)} %pad_clamp_fusion.2), kind=kCustom, calls=%fused_computation.1.clone | custom fusion | bytes 532496 | tf_op jit(solution)/shard_map/jit(_take)/gather | solution.py:162
  99.3 2.0 %maximum_select_fusion.1 = bf16[8,65,4,128]{3,1,2,0:T(8,128)(2,1)} fusion(bf16[4,65,4,128]{3,1,2,0:T(8,128)(2,1)} %collective-permute-done.7, bf16[4,1,4,128]{3,1,2,0:T(2,128)(2,1)S(1)} %copy-done.10, bf16[4,64,4,128]{3,1,2,0:T(8,128)(2,1)S(1)} %get-tuple-element.78, pred[]{:T(512)S(6)} %eq.4), kind=kLoop, calls=%fused_computation.20 | loop fusion | flops 3461120 | bytes 1064961 | tf_op jit(solution)/shard_map/jit(_where)/select_n | solution.py:73
  101.3 2.5 %gather_fusion.3 = bf16[4,65,4,128]{3,1,2,0:T(8,128)(2,1)} fusion(bf16[8,65,4,128]{3,1,2,0:T(8,128)(2,1)} %maximum_select_fusion.1, s32[1024]{0:T(1024)} %pad_clamp_fusion.2), kind=kCustom, calls=%fused_computation.5.clone | custom fusion | bytes 532496 | tf_op jit(solution)/shard_map/jit(_take)/gather | solution.py:167
  115.6 2.2 %maximum_select_fusion.2 = bf16[8,66,4,128]{3,1,2,0:T(8,128)(2,1)} fusion(bf16[4,66,4,128]{3,1,2,0:T(8,128)(2,1)} %collective-permute-done.8, bf16[4,1,4,128]{3,1,2,0:T(2,128)(2,1)S(1)} %copy-done.9, bf16[4,65,4,128]{3,1,2,0:T(8,128)(2,1)} %copy-done.1, pred[]{:T(512)S(6)} %eq.4), kind=kLoop, calls=%fused_computation.21 | loop fusion | flops 3514368 | bytes 1081345 | tf_op jit(solution)/shard_map/jit(_where)/select_n | solution.py:73
  117.8 2.5 %gather_fusion.4 = bf16[4,66,4,128]{3,1,2,0:T(8,128)(2,1)} fusion(bf16[8,66,4,128]{3,1,2,0:T(8,128)(2,1)} %maximum_select_fusion.2, s32[1024]{0:T(1024)} %pad_clamp_fusion.1), kind=kCustom, calls=%fused_computation.2.clone | custom fusion | bytes 540688 | tf_op jit(solution)/shard_map/jit(_take)/gather | solution.py:162
  120.3 2.0 %maximum_select_fusion.3 = bf16[8,66,4,128]{3,1,2,0:T(8,128)(2,1)} fusion(bf16[4,66,4,128]{3,1,2,0:T(8,128)(2,1)} %collective-permute-done.9, bf16[4,1,4,128]{3,1,2,0:T(2,128)(2,1)S(1)} %copy-done.8, bf16[4,65,4,128]{3,1,2,0:T(8,128)(2,1)S(1)} %get-tuple-element.76, pred[]{:T(512)S(6)} %eq.4), kind=kLoop, calls=%fused_computation.22 | loop fusion | flops 3514368 | bytes 1081345 | tf_op jit(solution)/shard_map/jit(_where)/select_n | solution.py:73
  122.4 2.5 %gather_fusion.5 = bf16[4,66,4,128]{3,1,2,0:T(8,128)(2,1)} fusion(bf16[8,66,4,128]{3,1,2,0:T(8,128)(2,1)} %maximum_select_fusion.3, s32[1024]{0:T(1024)} %pad_clamp_fusion.1), kind=kCustom, calls=%fused_computation.6.clone | custom fusion | bytes 540688 | tf_op jit(solution)/shard_map/jit(_take)/gather | solution.py:167
  135.7 2.2 %maximum_select_fusion.4 = bf16[8,67,4,128]{3,1,2,0:T(8,128)(2,1)} fusion(bf16[4,67,4,128]{3,1,2,0:T(8,128)(2,1)} %collective-permute-done.10, bf16[4,1,4,128]{3,1,2,0:T(2,128)(2,1)S(1)} %copy.202, bf16[4,66,4,128]{3,1,2,0:T(8,128)(2,1)} %copy-done.2, pred[]{:T(512)S(6)} %eq.4), kind=kLoop, calls=%fused_computation.23 | loop fusion | flops 3567616 | bytes 1097729 | tf_op jit(solution)/shard_map/jit(_where)/select_n | solution.py:73
  137.9 2.5 %gather_fusion.6 = bf16[4,67,4,128]{3,1,2,0:T(8,128)(2,1)} fusion(bf16[8,67,4,128]{3,1,2,0:T(8,128)(2,1)} %maximum_select_fusion.4, s32[1024]{0:T(1024)} %pad_clamp_fusion), kind=kCustom, calls=%fused_computation.3.clone | custom fusion | bytes 548880 | tf_op jit(solution)/shard_map/jit(_take)/gather | solution.py:162
  140.4 2.0 %maximum_select_fusion.5 = bf16[8,67,4,128]{3,1,2,0:T(8,128)(2,1)} fusion(bf16[4,67,4,128]{3,1,2,0:T(8,128)(2,1)} %collective-permute-done.11, bf16[4,1,4,128]{3,1,2,0:T(2,128)(2,1)S(1)} %broadcast_in_dim_squeeze.34, bf16[4,66,4,128]{3,1,2,0:T(8,128)(2,1)S(1)} %get-tuple-element.74, pred[]{:T(512)S(6)} %eq.4), kind=kLoop, calls=%fused_computation.24 | loop fusion | flops 3567616 | bytes 1097729 | tf_op jit(solution)/shard_map/jit(_where)/select_n | solution.py:73
  151.0 4.4 %fusion = bf16[3072,16]{0,1:T(8,128)(2,1)} fusion(bf16[1024,3072]{1,0:T(8,128)(2,1)} %param.25, bf16[4,1024]{1,0:T(4,128)(2,1)S(1)} %bitcast.85, bf16[4,1024]{1,0:T(4,128)(2,1)S(1)} %bitcast.86, bf16[4,1024]{1,0:T(4,128)(2,1)S(1)} %bitcast.87, bf16[4,1024]{1,0:T(4,128)(2,1)S(1)} %bitcast.84), kind=kOutput, calls=%fused_computation.9 | convolution fusion | flops 100843520 | bytes 6422528 | tf_op jit(solution)/shard_map/dot_general | solution.py:175
  155.3 9.1 %reduce-scatter.2.cloned.1.call-done = bf16[1536,16]{0,1:T(8,128)(2,1)} async-done(((bf16[3072,16]{0,1:T(8,128)(2,1)}), bf16[1536,16]{0,1:T(8,128)(2,1)}) %reduce-scatter.2.cloned.1.call-update) | async-done | bytes 49168 | tf_op jit(solution)/shard_map/reduce_scatter | solution.py:174
  (175 shorter events, 79.7 us)
Async XLA Ops:
  6.5 40.8 %copy-start = (bf16[3072,512]{1,0:T(8,128)(2,1)S(1)}, bf16[3072,512]{1,0:T(8,128)(2,1)}, u32[]{:S(2)}) copy-start(bf16[3072,512]{1,0:T(8,128)(2,1)} %param.24) | copy-start | bytes 9437188
  6.5 8.4 %copy-start.19 = (f32[3072]{0:T(1024)S(1)}, f32[3072]{0:T(1024)}, u32[]{:S(2)}) copy-start(f32[3072]{0:T(1024)} %param.21) | copy-start | bytes 36868
  6.5 10.1 %copy-start.24 = (s32[8]{0:T(128)S(1)}, s32[8]{0:T(128)}, u32[]{:S(2)}) copy-start(s32[8]{0:T(128)} %param.30) | copy-start | bytes 100
  6.5 157.9 %reduce-scatter.2.cloned.1.call-start = ((), (), s32[]{:S(2)}) async-start(), calls=%async_computation.1 | async-start | bytes 147456 | tf_op jit(solution)/shard_map/reduce_scatter | solution.py:174
  8.4 64.6 %collective-permute-start.3 = (bf16[4,64,4,128]{3,1,2,0:T(8,128)(2,1)}, bf16[4,64,4,128]{3,1,2,0:T(8,128)(2,1)}, u32[]{:S(2)}, u32[]{:S(2)}) collective-permute-start(bf16[4,64,4,128]{3,1,2,0:T(8,128)(2,1)} %copy_bitcast_fusion.1), channel_id=1, source_target_pairs={{0,2},{2,0},{4,6},{6,4},{8,10},{10,8},{12,14},{14,12},{16,18},{18,... | collective-permute-start | bytes 786440 | tf_op jit(solution)/shard_map/ppermute | solution.py:17
  12.4 65.2 %collective-permute-start.4 = (bf16[4,64,4,128]{3,1,2,0:T(8,128)(2,1)S(1)}, bf16[4,64,4,128]{3,1,2,0:T(8,128)(2,1)}, u32[]{:S(2)}, u32[]{:S(2)}) collective-permute-start(bf16[4,64,4,128]{3,1,2,0:T(8,128)(2,1)S(1)} %copy_bitcast_fusion), channel_id=1, source_target_pairs={{0,2},{2,0},{4,6},{6,4},{8,10},{10,8},{12,14},{14,12},{16,18},{18,... | collective-permute-start | bytes 786440 | tf_op jit(solution)/shard_map/ppermute | solution.py:17
  32.7 27.9 %collective-permute-start = (bf16[16,4,2,128]{3,0,2,1:T(8,128)(2,1)}, bf16[16,4,2,128]{3,0,2,1:T(8,128)(2,1)}, u32[]{:S(2)}, u32[]{:S(2)}) collective-permute-start(bf16[16,4,2,128]{3,0,2,1:T(8,128)(2,1)} %pad_maximum_fusion.6), channel_id=1, source_target_pairs={{0,2},{2,0},{4,6},{6,4},{8,10},{10,8},{12,14},{14,12},{16,18},{18,... | collective-permute-start | bytes 98312 | tf_op jit(solution)/shard_map/ppermute | solution.py:17
  48.7 12.0 %copy-start.6 = (bf16[16,8,64]{2,0,1:T(8,128)(2,1)S(1)}, bf16[16,8,64]{2,0,1:T(8,128)(2,1)}, u32[]{:S(2)}) copy-start(bf16[16,8,64]{2,0,1:T(8,128)(2,1)} %copy-done.5) | copy-start | bytes 49156
  63.4 5.2 %collective-permute-start.5 = (f32[16,4,2]{1,0,2:T(8,128)S(1)}, f32[16,4,2]{1,0,2:T(8,128)}, u32[]{:S(2)}, u32[]{:S(2)}) collective-permute-start(f32[16,4,2]{1,0,2:T(8,128)S(1)} %copy.233), channel_id=1, source_target_pairs={{0,2},{2,0},{4,6},{6,4},{8,10},{10,8},{12,14},{14,12},{16,18},{18,... | collective-permute-start | bytes 1544 | tf_op jit(solution)/shard_map/ppermute | solution.py:17
  63.5 5.0 %collective-permute-start.1 = (f32[16,4,2]{1,0,2:T(8,128)S(1)}, f32[16,4,2]{1,0,2:T(8,128)}, u32[]{:S(2)}, u32[]{:S(2)}) collective-permute-start(f32[16,4,2]{1,0,2:T(8,128)S(1)} %copy.231), channel_id=1, source_target_pairs={{0,2},{2,0},{4,6},{6,4},{8,10},{10,8},{12,14},{14,12},{16,18},{18,... | collective-permute-start | bytes 1544 | tf_op jit(solution)/shard_map/ppermute | solution.py:17
  67.7 4.4 %collective-permute-start.2 = (f32[16,4,2,128]{3,0,2,1:T(8,128)S(1)}, f32[16,4,2,128]{3,0,2,1:T(8,128)}, u32[]{:S(2)}, u32[]{:S(2)}) collective-permute-start(f32[16,4,2,128]{3,0,2,1:T(8,128)S(1)} %slice.185), channel_id=1, source_target_pairs={{0,2},{2,0},{4,6},{6,4},{8,10},{10,8},{12,14},{14,12},{16,18},{18,... | collective-permute-start | bytes 196616 | tf_op jit(solution)/shard_map/ppermute | solution.py:17
  75.1 6.9 %copy-start.23 = (pred[4]{0:T(512)(128)(4,1)S(1)}, pred[4]{0:T(512)(128)(4,1)}, u32[]{:S(2)}) copy-start(pred[4]{0:T(512)(128)(4,1)} %get-tuple-element.31) | copy-start | bytes 16
  77.6 5.6 %copy-start.11 = (bf16[4,1,4,128]{3,1,2,0:T(2,128)(2,1)S(1)}, bf16[4,1,4,128]{3,1,2,0:T(2,128)(2,1)}, u32[]{:S(2)}) copy-start(bf16[4,1,4,128]{3,1,2,0:T(2,128)(2,1)} %copy.177) | copy-start | bytes 12292
  84.3 10.3 %collective-permute-start.6 = (bf16[4,65,4,128]{3,1,2,0:T(8,128)(2,1)}, bf16[4,65,4,128]{3,1,2,0:T(8,128)(2,1)}, u32[]{:S(2)}, u32[]{:S(2)}) collective-permute-start(bf16[4,65,4,128]{3,1,2,0:T(8,128)(2,1)} %pad_maximum_fusion), channel_id=1, source_target_pairs={{0,2},{2,0},{4,6},{6,4},{8,10},{10,8},{12,14},{14,12},{16,18},{18,... | collective-permute-start | bytes 798728 | tf_op jit(solution)/shard_map/ppermute | solution.py:17
  87.3 12.0 %collective-permute-start.7 = (bf16[4,65,4,128]{3,1,2,0:T(8,128)(2,1)}, bf16[4,65,4,128]{3,1,2,0:T(8,128)(2,1)}, u32[]{:S(2)}, u32[]{:S(2)}) collective-permute-start(bf16[4,65,4,128]{3,1,2,0:T(8,128)(2,1)} %pad_maximum_fusion.1), channel_id=1, source_target_pairs={{0,2},{2,0},{4,6},{6,4},{8,10},{10,8},{12,14},{14,12},{16,18},{18,... | collective-permute-start | bytes 798728 | tf_op jit(solution)/shard_map/ppermute | solution.py:17
  96.8 7.0 %copy-start.22 = (pred[4]{0:T(512)(128)(4,1)S(1)}, pred[4]{0:T(512)(128)(4,1)}, u32[]{:S(2)}) copy-start(pred[4]{0:T(512)(128)(4,1)} %get-tuple-element.29) | copy-start | bytes 16
  99.3 6.5 %copy-start.9 = (bf16[4,1,4,128]{3,1,2,0:T(2,128)(2,1)S(1)}, bf16[4,1,4,128]{3,1,2,0:T(2,128)(2,1)}, u32[]{:S(2)}) copy-start(bf16[4,1,4,128]{3,1,2,0:T(2,128)(2,1)} %copy.192) | copy-start | bytes 12292
  101.3 5.8 %copy-start.8 = (bf16[4,1,4,128]{3,1,2,0:T(2,128)(2,1)S(1)}, bf16[4,1,4,128]{3,1,2,0:T(2,128)(2,1)}, u32[]{:S(2)}) copy-start(bf16[4,1,4,128]{3,1,2,0:T(2,128)(2,1)} %broadcast_in_dim_squeeze.33) | copy-start | bytes 12292
  106.5 9.1 %collective-permute-start.8 = (bf16[4,66,4,128]{3,1,2,0:T(8,128)(2,1)}, bf16[4,66,4,128]{3,1,2,0:T(8,128)(2,1)}, u32[]{:S(2)}, u32[]{:S(2)}) collective-permute-start(bf16[4,66,4,128]{3,1,2,0:T(8,128)(2,1)} %pad_maximum_fusion.2), channel_id=1, source_target_pairs={{0,2},{2,0},{4,6},{6,4},{8,10},{10,8},{12,14},{14,12},{16,18},{18,... | collective-permute-start | bytes 811016 | tf_op jit(solution)/shard_map/ppermute | solution.py:17
  107.9 12.4 %collective-permute-start.9 = (bf16[4,66,4,128]{3,1,2,0:T(8,128)(2,1)}, bf16[4,66,4,128]{3,1,2,0:T(8,128)(2,1)}, u32[]{:S(2)}, u32[]{:S(2)}) collective-permute-start(bf16[4,66,4,128]{3,1,2,0:T(8,128)(2,1)} %pad_maximum_fusion.3), channel_id=1, source_target_pairs={{0,2},{2,0},{4,6},{6,4},{8,10},{10,8},{12,14},{14,12},{16,18},{18,... | collective-permute-start | bytes 811016 | tf_op jit(solution)/shard_map/ppermute | solution.py:17
  117.8 7.0 %copy-start.21 = (pred[4]{0:T(512)(128)(4,1)S(1)}, pred[4]{0:T(512)(128)(4,1)}, u32[]{:S(2)}) copy-start(pred[4]{0:T(512)(128)(4,1)} %get-tuple-element.27) | copy-start | bytes 16
  127.5 8.2 %collective-permute-start.10 = (bf16[4,67,4,128]{3,1,2,0:T(8,128)(2,1)}, bf16[4,67,4,128]{3,1,2,0:T(8,128)(2,1)}, u32[]{:S(2)}, u32[]{:S(2)}) collective-permute-start(bf16[4,67,4,128]{3,1,2,0:T(8,128)(2,1)} %pad_maximum_fusion.4), channel_id=1, source_target_pairs={{0,2},{2,0},{4,6},{6,4},{8,10},{10,8},{12,14},{14,12},{16,18},{18,... | collective-permute-start | bytes 823304 | tf_op jit(solution)/shard_map/ppermute | solution.py:17
  130.0 10.4 %collective-permute-start.11 = (bf16[4,67,4,128]{3,1,2,0:T(8,128)(2,1)}, bf16[4,67,4,128]{3,1,2,0:T(8,128)(2,1)}, u32[]{:S(2)}, u32[]{:S(2)}) collective-permute-start(bf16[4,67,4,128]{3,1,2,0:T(8,128)(2,1)} %pad_maximum_fusion.5), channel_id=1, source_target_pairs={{0,2},{2,0},{4,6},{6,4},{8,10},{10,8},{12,14},{14,12},{16,18},{18,... | collective-permute-start | bytes 823304 | tf_op jit(solution)/shard_map/ppermute | solution.py:17
  144.2 6.6 %copy-start.16 = (f32[4,4,2,128]{3,2,1,0:T(2,128)S(1)}, f32[4,4,2,128]{3,2,1,0:T(2,128)}, u32[]{:S(2)}) copy-start(f32[4,4,2,128]{3,2,1,0:T(2,128)} %fusion.59) | copy-start | bytes 49156
  (14 other events, 42.2 us)
Sparse Core Ops, SparseCore 0:
  155.5 8.9 reduce-scatter.1
where the time goes:
time: 175 us; the launch traced here: 173 us
  local copies, waits for them, and re-layouts  59.4 us (34%)
  other arithmetic  40.6 us (23%)
  matrix products  26.3 us (15%)
  waiting for transfers between devices  16.6 us (9%)
  between operations  14.4 us (8%)
  starting transfers between devices  13.2 us (8%)
  blocking collectives  2.28 us (1%)
    select_n x8, other arithmetic, in_order(): jnp.where(parity == 0, jnp.concatenate([mine, partner], axis=0), jnp.conc...  16.9 us
    ppermute x12, starting transfers between devices, from_partner(): return lax.ppermute(value, axis, pairs)  13.2 us
    gather x4, local copies, waits for them, and re-layouts, body(): jnp.take(in_order(hist_k, other_k, parity), chosen, axis=0)  9.9 us
    gather x4, local copies, waits for them, and re-layouts, body(): jnp.take(in_order(hist_v, other_v, parity), chosen, axis=0)  9.27 us
    reduce_scatter x1, waiting for transfers between devices, body(): lax.psum_scatter(lax.dot_general(w_out, context_all, (((0,), (1,)), ((),...  9.14 us
    dot_general x1, local copies, waits for them, and re-layouts, body(): jnp.dot(normed, w_query, preferred_element_type=jnp.float32)  8.63 us
    ppermute x12, waiting for transfers between devices, from_partner(): return lax.ppermute(value, axis, pairs)  7.43 us
    dot_general x4, matrix products, history_partial(): jnp.einsum('bkgt,btkd->bkgd', weights.astype(jnp.bfloat16), hist_v, prefe...  5.74 us
  transfers between devices with their start and end apart: 13, of which 5 were waited for; matrix products, arithmetic and copies ran while one was open for 50% of the time, Pallas kernels for 0%

commit v1 on v0

v1 whole, which is shorter than its diff:
```python
import functools
import math

import jax
import jax.numpy as jnp
from jax import lax
from jax.experimental import pallas as pl
from jax.experimental.pallas import tpu as pltpu
from jax.sharding import PartitionSpec as P

HD = 128
BEAMS = 8

norm_eps = 1e-05
masked_score = -1e30
rope_base = 500000.0


def permute_by(value, axis, distance):
    pairs = [(source, source ^ distance) for source in range(lax.axis_size(axis))]
    return lax.ppermute(value, axis, pairs)


def across(value, beam_distance, tp_distance):
    req, tp = lax.axis_size("req"), lax.axis_size("tp")
    pairs = [
        (r * tp + t, (r ^ beam_distance) * tp + (t ^ tp_distance))
        for r in range(req)
        for t in range(tp)
    ]
    return lax.ppermute(value, ("req", "tp"), pairs)


def attend_kernel(
    sizes, lengths_ref, parents_ref, gain_ref, inverse_ref, *refs
):
    steps, own, tp, kv, group, half_len, history = sizes
    pieces = refs[: 2 * tp]
    (wq, wk, wv, pk, pv, gk, gv, kept_ref, kept_lse_ref, sent_ref) = refs[2 * tp : 2 * tp + 10]
    (x_s, xn_s, w_s, pk_s, pv_s, gk_s, gv_s, q_s, k_s, v_s, sems) = refs[2 * tp + 10 :]
    rows = steps * own
    part = pieces[0].shape[-1]
    qw = group * HD
    device = lax.axis_index("req")
    request = device // 2
    parity = device % 2
    me_tp = lax.axis_index("tp")

    copies = []
    for g in range(kv):
        copies.append(
            [
                pltpu.make_async_copy(
                    wq.at[:, pl.ds(g * qw, qw)], w_s.at[g, :, pl.ds(0, qw)], sems.at[3 * g]
                ),
                pltpu.make_async_copy(
                    wk.at[:, pl.ds(g * HD, HD)], w_s.at[g, :, pl.ds(qw, HD)], sems.at[3 * g + 1]
                ),
                pltpu.make_async_copy(
                    wv.at[:, pl.ds(g * HD, HD)],
                    w_s.at[g, :, pl.ds(qw + HD, HD)],
                    sems.at[3 * g + 2],
                ),
            ]
        )
    cache_copies = [
        pltpu.make_async_copy(source, target, sems.at[3 * kv + n])
        for n, (source, target) in enumerate(((pk, pk_s), (pv, pv_s), (gk, gk_s), (gv, gv_s)))
    ]
    for group_copies in copies:
        for copy in group_copies:
            copy.start()
    for copy in cache_copies:
        copy.start()

    squares = []
    for b in range(2):
        total = jnp.zeros((rows, HD), jnp.float32)
        for t in range(tp):
            block = me_tp ^ t
            column = pl.multiple_of(block * part, HD)
            for s in range(steps):
                x_s[pl.ds(b * rows + s * own, own), pl.ds(column, part)] = pieces[b * tp + t][
                    s
                ].astype(jnp.float32)
            mine = x_s[pl.ds(b * rows, rows), pl.ds(column, part)]
            mine = mine * mine
            for c in range(part // HD):
                total = total + mine[:, c * HD : (c + 1) * HD]
        squares.append(jnp.sum(total, axis=-1, keepdims=True))
    width = part * tp
    scale = lax.rsqrt(jnp.concatenate(squares, axis=0) / width + norm_eps)
    xn_s[...] = (x_s[...] * scale * gain_ref[...]).astype(jnp.bfloat16)

    length = lengths_ref[request]
    row = lax.broadcasted_iota(jnp.int32, (2 * rows, HD), 0)
    step = (row % rows) // own
    angle = (length + history + step).astype(jnp.float32) * inverse_ref[...]
    lane = lax.broadcasted_iota(jnp.int32, (2 * rows, HD), 1)
    cosine = jnp.cos(angle)
    sine = jnp.where(lane < HD // 2, -jnp.sin(angle), jnp.sin(angle))

    def rotate(x):
        return x * cosine + pltpu.roll(x, HD // 2, 1) * sine

    count = group * 2 * rows

    def parent_of(s, beam):
        out = jnp.zeros_like(beam)
        for j in range(BEAMS):
            out = jnp.where(beam == j, parents_ref[s, request * BEAMS + j], out)
        return out

    row = lax.broadcasted_iota(jnp.int32, (count, HD), 0) % (2 * rows)
    row_step = (row % rows) // own
    row_parity = jnp.where(row < rows, parity, 1 - parity)
    beam = row_parity * own + row % own
    ancestors = [None] * steps
    at = beam
    for s in reversed(range(steps)):
        if s < steps - 1:
            at = jnp.where(row_step > s, parent_of(s + 1, at), beam)
        ancestors[s] = jnp.where(row_step >= s, at, -1)
    origin = parent_of(0, at)
    lane = lax.broadcasted_iota(jnp.int32, (count, HD), 1)

    zero = jnp.zeros((count, HD), jnp.float32)
    gen_bias = []
    per = HD // history if history < HD else 1
    for c in range(own * history // HD):
        key_beam = parity * own + (c * HD + lane) // history
        gen_bias.append(jnp.where(key_beam == origin, zero, masked_score))
    gen_bias = jnp.concatenate(gen_bias, axis=1)
    new_bias = zero + masked_score
    for s in range(steps):
        hit = (lane // own == s) & (ancestors[s] == parity * own + lane % own)
        new_bias = jnp.where(hit, 0.0, new_bias)
    new_bias = new_bias[:, :rows]
    place = parity * half_len + lax.broadcasted_iota(jnp.int32, (1, half_len), 1)
    prompt_bias = jnp.where(place < length, 0.0, masked_score)

    for g in range(kv):
        for copy in copies[g]:
            copy.wait()
        out = jnp.dot(xn_s[...], w_s[g], preferred_element_type=jnp.float32)
        for j in range(group):
            q_s[g, pl.ds(j * 2 * rows, 2 * rows), :] = rotate(
                out[:, j * HD : (j + 1) * HD]
            ).astype(jnp.bfloat16)
        k_s[g] = rotate(out[:, qw : qw + HD]).astype(jnp.bfloat16)
        v_s[g] = out[:, qw + HD :].astype(jnp.bfloat16)
    for copy in cache_copies:
        copy.wait()

    scaling = HD**-0.5
    contract = (((1,), (1,)), ((), ()))
    lse_lane = lax.broadcasted_iota(jnp.int32, (rows, HD), 1)
    kept_lse = jnp.zeros((rows, HD), jnp.float32)
    sent_lse = jnp.zeros((rows, HD), jnp.float32)
    for g in range(kv):
        cols = pl.ds(g * HD, HD)
        q = q_s[g]
        s_prompt = (
            lax.dot_general(q, pk_s[0, :, cols], contract, preferred_element_type=jnp.float32)
            * scaling
            + prompt_bias
        )
        s_gen = (
            lax.dot_general(
                q,
                gk_s[:, :, cols].reshape(own * history, HD),
                contract,
                preferred_element_type=jnp.float32,
            )
            * scaling
            + gen_bias
        )
        s_new = (
            lax.dot_general(
                q, k_s[g, pl.ds(0, rows), :], contract, preferred_element_type=jnp.float32
            )
            * scaling
            + new_bias
        )
        top = jnp.maximum(
            jnp.maximum(
                jnp.max(s_prompt, axis=-1, keepdims=True), jnp.max(s_gen, axis=-1, keepdims=True)
            ),
            jnp.max(s_new, axis=-1, keepdims=True),
        )
        e_prompt = jnp.exp(s_prompt - top)
        e_gen = jnp.exp(s_gen - top)
        e_new = jnp.exp(s_new - top)
        total = (
            jnp.sum(e_prompt, axis=-1, keepdims=True)
            + jnp.sum(e_gen, axis=-1, keepdims=True)
            + jnp.sum(e_new, axis=-1, keepdims=True)
        )
        mixed = (
            jnp.dot(
                e_prompt.astype(jnp.bfloat16),
                pv_s[0, :, cols],
                preferred_element_type=jnp.float32,
            )
            + jnp.dot(
                e_gen.astype(jnp.bfloat16),
                gv_s[:, :, cols].reshape(own * history, HD),
                preferred_element_type=jnp.float32,
            )
            + jnp.dot(
                e_new.astype(jnp.bfloat16),
                v_s[g, pl.ds(0, rows), :],
                preferred_element_type=jnp.float32,
            )
        )
        mixed = mixed / total
        lse = top + jnp.log(total)
        for j in range(group):
            h = g * group + j
            lower = j * 2 * rows
            kept_ref[:, pl.ds(h * HD, HD)] = mixed[lower : lower + rows]
            sent_ref[:, pl.ds(h * HD, HD)] = mixed[lower + rows : lower + 2 * rows].astype(
                jnp.bfloat16
            )
            kept_lse = jnp.where(lse_lane == h, lse[lower : lower + rows], kept_lse)
            sent_lse = jnp.where(lse_lane == h, lse[lower + rows : lower + 2 * rows], sent_lse)
    kept_lse_ref[...] = kept_lse
    base = kv * group * HD
    rest = sent_lse
    for n in range(3):
        term = rest.astype(jnp.bfloat16)
        sent_ref[:, pl.ds(base + n * HD, HD)] = term
        rest = rest - term.astype(jnp.float32)


def project_kernel(sizes, kept_ref, kept_lse_ref, got_ref, w_out, *refs):
    steps, own, tp, heads, chunk = sizes
    outs = refs[:tp]
    w_s, ctx_s, sems = refs[tp:]
    me_tp = lax.axis_index("tp")
    part = outs[0].shape[-1]
    per = part // chunk
    copies = []
    for d in list(range(1, tp)) + [0]:
        for c in range(per):
            column = pl.multiple_of((me_tp ^ d) * part + c * chunk, HD)
            slot = d * per + c
            copies.append(
                (
                    d,
                    c,
                    slot,
                    pltpu.make_async_copy(
                        w_out.at[:, pl.ds(column, chunk)], w_s.at[slot], sems.at[slot]
                    ),
                )
            )
    for _, _, _, copy in copies:
        copy.start()
    base = heads * HD
    lse_mine = kept_lse_ref[...]
    lse_got = (
        got_ref[:, pl.ds(base, HD)].astype(jnp.float32)
        + got_ref[:, pl.ds(base + HD, HD)].astype(jnp.float32)
        + got_ref[:, pl.ds(base + 2 * HD, HD)].astype(jnp.float32)
    )
    top = jnp.maximum(lse_mine, lse_got)
    mine = jnp.exp(lse_mine - top)
    got = jnp.exp(lse_got - top)
    share = mine / (mine + got)
    for h in range(heads):
        cols = pl.ds(h * HD, HD)
        w = share[:, h : h + 1]
        ctx_s[:, cols] = (
            kept_ref[:, cols] * w + got_ref[:, cols].astype(jnp.float32) * (1.0 - w)
        ).astype(jnp.bfloat16)
    for d, c, slot, copy in copies:
        copy.wait()
        out = jnp.dot(ctx_s[...], w_s[slot], preferred_element_type=jnp.float32)
        for s in range(steps):
            outs[d][s, :, pl.ds(c * chunk, chunk)] = out[s * own : (s + 1) * own].astype(
                outs[d].dtype
            )


def body(
    hidden_in,
    norm_gain,
    w_query,
    w_key,
    w_value,
    w_out,
    prompt_keys,
    prompt_values,
    gen_keys,
    gen_values,
    lengths,
    parents,
):
    steps, own, part = hidden_in.shape
    tp = lax.axis_size("tp")
    rows = steps * own
    width = w_query.shape[0]
    kv = w_key.shape[1] // HD
    group = w_query.shape[1] // w_key.shape[1]
    heads = kv * group
    half_len = prompt_keys.shape[1]
    history = gen_keys.shape[1]

    pieces = [
        hidden_in if (b, t) == (0, 0) else across(hidden_in, b, t)
        for b in range(2)
        for t in range(tp)
    ]
    half_dim = HD // 2
    inverse = rope_base ** (-jnp.arange(half_dim, dtype=jnp.float32) / half_dim)
    inverse = jnp.concatenate([inverse, inverse])[None, :]

    smem = pl.BlockSpec(memory_space=pltpu.SMEM)
    vmem = pl.BlockSpec(memory_space=pltpu.VMEM)
    hbm = pl.BlockSpec(memory_space=pl.ANY)
    sizes = (steps, own, tp, kv, group, half_len, history)
    kept, kept_lse, sent = pl.pallas_call(
        functools.partial(attend_kernel, sizes),
        out_shape=(
            jax.ShapeDtypeStruct((rows, heads * HD), jnp.float32),
            jax.ShapeDtypeStruct((rows, HD), jnp.float32),
            jax.ShapeDtypeStruct((rows, heads * HD + 3 * HD), jnp.bfloat16),
        ),
        in_specs=[smem, smem, vmem, vmem] + [vmem] * (2 * tp) + [hbm] * 7,
        out_specs=(vmem, vmem, vmem),
        scratch_shapes=[
            pltpu.VMEM((2 * rows, width), jnp.float32),
            pltpu.VMEM((2 * rows, width), jnp.bfloat16),
            pltpu.VMEM((kv, width, (group + 2) * HD), jnp.bfloat16),
            pltpu.VMEM(prompt_keys.shape, jnp.bfloat16),
            pltpu.VMEM(prompt_values.shape, jnp.bfloat16),
            pltpu.VMEM(gen_keys.shape, jnp.bfloat16),
            pltpu.VMEM(gen_values.shape, jnp.bfloat16),
            pltpu.VMEM((kv, group * 2 * rows, HD), jnp.bfloat16),
            pltpu.VMEM((kv, 2 * rows, HD), jnp.bfloat16),
            pltpu.VMEM((kv, 2 * rows, HD), jnp.bfloat16),
            pltpu.SemaphoreType.DMA((3 * kv + 4,)),
        ],
        compiler_params=pltpu.CompilerParams(vmem_limit_bytes=40 * 2**20),
        name="attend",
    )(
        lengths,
        parents,
        norm_gain[None, :],
        inverse,
        *pieces,
        w_query,
        w_key,
        w_value,
        prompt_keys,
        prompt_values,
        gen_keys,
        gen_values,
    )

    got = permute_by(sent, "req", 1)

    chunk = math.gcd(part, 512)
    out_types = [jnp.float32] + [jnp.bfloat16] * (tp - 1)
    sums = pl.pallas_call(
        functools.partial(project_kernel, (steps, own, tp, heads, chunk)),
        out_shape=tuple(jax.ShapeDtypeStruct((steps, own, part), kind) for kind in out_types),
        in_specs=[vmem, vmem, vmem, hbm],
        out_specs=(vmem,) * tp,
        scratch_shapes=[
            pltpu.VMEM((width // chunk, heads * HD, chunk), jnp.bfloat16),
            pltpu.VMEM((rows, heads * HD), jnp.bfloat16),
            pltpu.SemaphoreType.DMA((width // chunk,)),
        ],
        compiler_params=pltpu.CompilerParams(vmem_limit_bytes=40 * 2**20),
        name="project",
    )(kept, kept_lse, got, w_out)
    total = sums[0]
    for t in range(1, tp):
        total = total + across(sums[t], 0, t).astype(jnp.float32)
    return total.astype(jnp.bfloat16)


def solution(mesh):
    in_specs = (
        P(None, "req", "tp"),
        P(),
        P(None, "tp"),
        P(None, "tp"),
        P(None, "tp"),
        P("tp", None),
        P("req", None, "tp"),
        P("req", None, "tp"),
        P("req", None, "tp"),
        P("req", None, "tp"),
        P(),
        P(),
    )
    out_specs = P(None, "req", "tp")
    return jax.shard_map(body, mesh=mesh, in_specs=in_specs, out_specs=out_specs, check_vma=False)
```

time: 175 us -> 36.7 us (0.21)
  local copies, waits for them, and re-layouts: 59.4 us -> 13.4 us
  other arithmetic: 40.6 us -> 0.73 us
  matrix products: 26.3 us -> 0 us
  between operations: 14.4 us -> 0.04 us
  Pallas kernels: 0 us -> 9.98 us
  starting transfers between devices: 13.2 us -> 4.13 us
  waiting for transfers between devices: 16.6 us -> 7.87 us
  blocking collectives: 2.28 us -> 0 us
    dot_general x14 -> x0, matrix products: 26.3 us -> none  [the longest x4 5.74 us: history_partial(): jnp.einsum('bkgt,btkd->bkgd', weights.astype(jnp.bfloat16), hist_v, prefe...]
    select_n x12 -> x0, other arithmetic: 22.2 us -> none  [the longest x8 16.9 us: in_order(): jnp.where(parity == 0, jnp.concatenate([mine, partner], axis=0), jnp.conc...]
    gather x8 -> x0, local copies, waits for them, and re-layouts: 19.2 us -> none  [the longest x4 9.9 us: body(): jnp.take(in_order(hist_k, other_k, parity), chosen, axis=0)]
    dot_general x2 -> x0, local copies, waits for them, and re-layouts: 13.3 us -> none  [the longest x1 8.63 us: body(): jnp.dot(normed, w_query, preferred_element_type=jnp.float32)]
    pallas_call x0 -> x2, Pallas kernels: none -> 9.98 us  [the longest x1 7.44 us: body(): pl.pallas_call(functools.partial(attend_kernel, sizes), out_shape=(jax.Sh...]
    unnamed x54 -> x24, local copies, waits for them, and re-layouts: 3.95 us -> 13.4 us
    reshape x6 -> x0, local copies, waits for them, and re-layouts: 9.29 us -> none  [the longest x2 2.46 us: body(): (inputs * inverse * norm_gain).astype(jnp.bfloat16).reshape(total_rows, -1)]
    reduce_scatter x1 -> x0, waiting for transfers between devices: 9.14 us -> none  [body(): lax.psum_scatter(lax.dot_general(w_out, context_all, (((0,), (1,)), ((),...]
  transfers between devices with their start and end apart: 13 -> 5, of which waited for: 5 -> 4; matrix products, arithmetic and copies ran while one was open for 50% -> 0% of each run, Pallas kernels for 0% -> 0%
where the time goes in v1:
time: 36.7 us; the launch traced here: 36.1 us
  local copies, waits for them, and re-layouts  13.4 us (37%)
  Pallas kernels  9.98 us (27%)
  waiting for transfers between devices  7.87 us (21%)
  starting transfers between devices  4.13 us (11%)
  other arithmetic  0.73 us (2%)
    unnamed x24, local copies, waits for them, and re-layouts  13.4 us
    pallas_call x1, Pallas kernels, body(): pl.pallas_call(functools.partial(attend_kernel, sizes), out_shape=(jax.Sh...  7.44 us
    ppermute x4, waiting for transfers between devices, across(): return lax.ppermute(value, ('req', 'tp'), pairs)  4.74 us
    ppermute x1, waiting for transfers between devices, permute_by(): return lax.ppermute(value, axis, pairs)  3.14 us
    ppermute x4, starting transfers between devices, across(): return lax.ppermute(value, ('req', 'tp'), pairs)  3.13 us
    pallas_call x1, Pallas kernels, body(): pl.pallas_call(functools.partial(project_kernel, (steps, own, tp, heads,...  2.54 us
    ppermute x1, starting transfers between devices, permute_by(): return lax.ppermute(value, axis, pairs)  1 us
  transfers between devices with their start and end apart: 5, of which 4 were waited for; matrix products, arithmetic and copies ran while one was open for 0% of the time, Pallas kernels for 0%

profile of v1, /device:TPU:0, one launch (start us, length us, event | category | flops | bytes accessed | tf_op | source)
XLA Modules:
  0.0 36.1 jit_solution(2662236275205653171)
XLA Ops:
  0.0 2.9 %collective-permute-start.1 = (bf16[4,4,1536]{2,1,0:T(4,128)(2,1)}, bf16[4,4,1536]{2,1,0:T(4,128)(2,1)S(1)}, u32[]{:S(2)}, u32[]{:S(2)}) collective-permute-start(bf16[4,4,1536]{2,1,0:T(4,128)(2,1)} %refs_0_.1), channel_id=1, source_target_pairs={{0,2},{1,3},{2,0},{3,1},{4,6},{5,7},{6,4},{7,5},{8,10},{9,11},{10,... | collective-permute-start | bytes 147464 | tf_op jit(solution)/shard_map/ppermute | solution.py:31
  2.9 0.0 collective-permute-start
  2.9 0.1 collective-permute-start.2
  3.1 0.1 maximum_bitcast_fusion.inverse_ref
  3.1 2.1 %collective-permute-done.1.refs_2_ = bf16[4,4,1536]{2,1,0:T(4,128)(2,1)S(1)} collective-permute-done((bf16[4,4,1536]{2,1,0:T(4,128)(2,1)}, bf16[4,4,1536]{2,1,0:T(4,128)(2,1)S(1)}, u32[]{:S(2)}, u32[]{:S(2)}) %collective-permute-start.1) | collective-permute-done | bytes 49184 | tf_op jit(solution)/shard_map/ppermute | solution.py:31
  5.2 1.4 %collective-permute-done.2.refs_3_ = bf16[4,4,1536]{2,1,0:T(4,128)(2,1)S(1)} collective-permute-done((bf16[4,4,1536]{2,1,0:T(4,128)(2,1)}, bf16[4,4,1536]{2,1,0:T(4,128)(2,1)S(1)}, u32[]{:S(2)}, u32[]{:S(2)}) %collective-permute-start.2) | collective-permute-done | bytes 49184 | tf_op jit(solution)/shard_map/ppermute | solution.py:31
  6.7 2.8 %copy-done.1 = bf16[3072,1024]{1,0:T(8,128)(2,1)S(1)} copy-done((bf16[3072,1024]{1,0:T(8,128)(2,1)S(1)}, bf16[3072,1024]{1,0:T(8,128)(2,1)}, u32[]{:S(2)}) %copy-start.1) | copy-done | bytes 6291480
  9.5 1.9 %copy-done.2 = bf16[3072,512]{1,0:T(8,128)(2,1)S(1)} copy-done((bf16[3072,512]{1,0:T(8,128)(2,1)S(1)}, bf16[3072,512]{1,0:T(8,128)(2,1)}, u32[]{:S(2)}) %copy-start.2) | copy-done | bytes 3145752
  11.3 1.9 %copy-done.3 = bf16[3072,512]{1,0:T(8,128)(2,1)S(1)} copy-done((bf16[3072,512]{1,0:T(8,128)(2,1)S(1)}, bf16[3072,512]{1,0:T(8,128)(2,1)}, u32[]{:S(2)}) %copy-start.3) | copy-done | bytes 3145752
  13.2 1.0 %copy-done.4 = bf16[1,512,512]{2,1,0:T(8,128)(2,1)S(1)} copy-done((bf16[1,512,512]{2,1,0:T(8,128)(2,1)S(1)}, bf16[1,512,512]{2,1,0:T(8,128)(2,1)}, u32[]{:S(2)}) %copy-start.4) | copy-done | bytes 524312
  14.3 1.0 %copy-done.5 = bf16[1,512,512]{2,1,0:T(8,128)(2,1)S(1)} copy-done((bf16[1,512,512]{2,1,0:T(8,128)(2,1)S(1)}, bf16[1,512,512]{2,1,0:T(8,128)(2,1)}, u32[]{:S(2)}) %copy-start.5) | copy-done | bytes 524312
  15.3 0.9 %copy-done.6 = bf16[4,64,512]{2,1,0:T(8,128)(2,1)S(1)} copy-done((bf16[4,64,512]{2,1,0:T(8,128)(2,1)S(1)}, bf16[4,64,512]{2,1,0:T(8,128)(2,1)}, u32[]{:S(2)}) %copy-start.6) | copy-done | bytes 262168
  16.3 0.9 %copy-done.7 = bf16[4,64,512]{2,1,0:T(8,128)(2,1)S(1)} copy-done((bf16[4,64,512]{2,1,0:T(8,128)(2,1)S(1)}, bf16[4,64,512]{2,1,0:T(8,128)(2,1)}, u32[]{:S(2)}) %copy-start.7) | copy-done | bytes 262168
  17.2 0.8 %copy-done.8 = bf16[4,4,1536]{2,1,0:T(4,128)(2,1)S(1)} copy-done((bf16[4,4,1536]{2,1,0:T(4,128)(2,1)S(1)}, bf16[4,4,1536]{2,1,0:T(4,128)(2,1)}, u32[]{:S(2)}) %copy-start.8) | copy-done | bytes 49176
  18.0 0.7 %copy-done.9 = f32[3072]{0:T(1024)S(1)} copy-done((f32[3072]{0:T(1024)S(1)}, f32[3072]{0:T(1024)}, u32[]{:S(2)}) %copy-start.9) | copy-done | bytes 12312
  18.7 0.7 %copy-done.10 = s32[4,64]{1,0:T(4,128)S(1)} copy-done((s32[4,64]{1,0:T(4,128)S(1)}, s32[4,64]{1,0:T(4,128)}, u32[]{:S(2)}) %copy-start.10) | copy-done | bytes 1048
  19.4 0.7 %copy-done.11 = s32[8]{0:T(128)S(1)} copy-done((s32[8]{0:T(128)S(1)}, s32[8]{0:T(128)}, u32[]{:S(2)}) %copy-start.11) | copy-done | bytes 56
  20.1 7.4 %attend.1 = (f32[16,1024]{1,0:T(8,128)S(1)}, f32[16,128]{1,0:T(8,128)S(1)}, bf16[16,1408]{1,0:T(8,128)(2,1)S(1)}) custom-call(s32[8]{0:T(128)S(1)} %copy-done.11, s32[4,64]{1,0:T(4,128)S(1)} %copy-done.10, f32[1,3072]{1,0:T(1,128)S(1)} %bitcast.3, f32[1,128]{1,0:T(1,128)S(1)} %maximum_bitcast_fusion.inverse_ref, bf16[4,4,1536]{2,1,0:T(4,128)(2,1)S(1)} %copy-done.8, ...), custom_call_target="tpu_custom_call" | custom-call | tf_op jit(solution)/shard_map/attend/pallas_call | solution.py:323
  27.5 1.0 %collective-permute-start.3 = (bf16[16,1408]{1,0:T(8,128)(2,1)S(1)}, bf16[16,1408]{1,0:T(8,128)(2,1)S(1)}, u32[]{:S(2)}, u32[]{:S(2)}) collective-permute-start(bf16[16,1408]{1,0:T(8,128)(2,1)S(1)} %get-tuple-element.12), channel_id=1, source_target_pairs={{0,2},{2,0},{4,6},{6,4},{8,10},{10,8},{12,14},{14,12},{16,18},{18,... | collective-permute-start | bytes 135176 | tf_op jit(solution)/shard_map/ppermute | solution.py:21
  28.5 3.1 %collective-permute-done.3.got_ref = bf16[16,1408]{1,0:T(8,128)(2,1)S(1)} collective-permute-done((bf16[16,1408]{1,0:T(8,128)(2,1)S(1)}, bf16[16,1408]{1,0:T(8,128)(2,1)S(1)}, u32[]{:S(2)}, u32[]{:S(2)}) %collective-permute-start.3) | collective-permute-done | bytes 45088 | tf_op jit(solution)/shard_map/ppermute | solution.py:21
  31.7 2.5 %project.1 = (f32[4,4,1536]{2,1,0:T(4,128)S(1)}, bf16[4,4,1536]{2,1,0:T(4,128)(2,1)S(1)}) custom-call(f32[16,1024]{1,0:T(8,128)S(1)} %get-tuple-element.10.kept_ref, f32[16,128]{1,0:T(8,128)S(1)} %get-tuple-element.11.kept_lse_ref, bf16[16,1408]{1,0:T(8,128)(2,1)S(1)} %collective-permute-done.3.got_ref, bf16[1024,3072]{1,0:T(8,128)(2,1)S(1)} %copy-done), custom_call_target="tpu_custom_call" | custom-call | tf_op jit(solution)/shard_map/project/pallas_call | solution.py:366
  34.2 0.1 collective-permute-start.4
  34.3 1.2 %collective-permute-done.4 = bf16[4,4,1536]{2,1,0:T(4,128)(2,1)S(1)} collective-permute-done((bf16[4,4,1536]{2,1,0:T(4,128)(2,1)S(1)}, bf16[4,4,1536]{2,1,0:T(4,128)(2,1)S(1)}, u32[]{:S(2)}, u32[]{:S(2)}) %collective-permute-start.4) | collective-permute-done | bytes 49184 | tf_op jit(solution)/shard_map/ppermute | solution.py:31
  35.5 0.6 %add_convert_fusion = bf16[4,4,1536]{2,1,0:T(4,128)(2,1)} fusion(f32[4,4,1536]{2,1,0:T(4,128)S(1)} %get-tuple-element.13, bf16[4,4,1536]{2,1,0:T(4,128)(2,1)S(1)} %collective-permute-done.4), kind=kLoop, calls=%fused_computation | loop fusion | flops 73728 | bytes 196608 | tf_op jit(solution)/shard_map/convert_element_type | solution.py:382
  (15 shorter events, 0.0 us)
Async XLA Ops:
  0.0 5.2 %collective-permute-start.1 = (bf16[4,4,1536]{2,1,0:T(4,128)(2,1)}, bf16[4,4,1536]{2,1,0:T(4,128)(2,1)S(1)}, u32[]{:S(2)}, u32[]{:S(2)}) collective-permute-start(bf16[4,4,1536]{2,1,0:T(4,128)(2,1)} %refs_0_.1), channel_id=1, source_target_pairs={{0,2},{1,3},{2,0},{3,1},{4,6},{5,7},{6,4},{7,5},{8,10},{9,11},{10,... | collective-permute-start | bytes 147464 | tf_op jit(solution)/shard_map/ppermute | solution.py:31
  2.9 2.3 %collective-permute-start = (bf16[4,4,1536]{2,1,0:T(4,128)(2,1)}, bf16[4,4,1536]{2,1,0:T(4,128)(2,1)S(1)}, u32[]{:S(2)}, u32[]{:S(2)}) collective-permute-start(bf16[4,4,1536]{2,1,0:T(4,128)(2,1)} %refs_0_.1), channel_id=1, source_target_pairs={{0,1},{1,0},{2,3},{3,2},{4,5},{5,4},{6,7},{7,6},{8,9},{9,8},{10,11... | collective-permute-start | bytes 147464 | tf_op jit(solution)/shard_map/ppermute | solution.py:31
  2.9 3.7 %collective-permute-start.2 = (bf16[4,4,1536]{2,1,0:T(4,128)(2,1)}, bf16[4,4,1536]{2,1,0:T(4,128)(2,1)S(1)}, u32[]{:S(2)}, u32[]{:S(2)}) collective-permute-start(bf16[4,4,1536]{2,1,0:T(4,128)(2,1)} %refs_0_.1), channel_id=1, source_target_pairs={{0,3},{1,2},{2,1},{3,0},{4,7},{5,6},{6,5},{7,4},{8,11},{9,10},{10,... | collective-permute-start | bytes 147464 | tf_op jit(solution)/shard_map/ppermute | solution.py:31
  6.7 2.8 %copy-start.1 = (bf16[3072,1024]{1,0:T(8,128)(2,1)S(1)}, bf16[3072,1024]{1,0:T(8,128)(2,1)}, u32[]{:S(2)}) copy-start(bf16[3072,1024]{1,0:T(8,128)(2,1)} %refs_4_.1) | copy-start | bytes 18874372
  9.5 1.9 %copy-start.2 = (bf16[3072,512]{1,0:T(8,128)(2,1)S(1)}, bf16[3072,512]{1,0:T(8,128)(2,1)}, u32[]{:S(2)}) copy-start(bf16[3072,512]{1,0:T(8,128)(2,1)} %refs_5_.1) | copy-start | bytes 9437188
  11.3 1.9 %copy-start.3 = (bf16[3072,512]{1,0:T(8,128)(2,1)S(1)}, bf16[3072,512]{1,0:T(8,128)(2,1)}, u32[]{:S(2)}) copy-start(bf16[3072,512]{1,0:T(8,128)(2,1)} %refs_6_.1) | copy-start | bytes 9437188
  13.2 1.0 %copy-start.4 = (bf16[1,512,512]{2,1,0:T(8,128)(2,1)S(1)}, bf16[1,512,512]{2,1,0:T(8,128)(2,1)}, u32[]{:S(2)}) copy-start(bf16[1,512,512]{2,1,0:T(8,128)(2,1)} %refs_7_.1) | copy-start | bytes 1572868
  14.3 1.0 %copy-start.5 = (bf16[1,512,512]{2,1,0:T(8,128)(2,1)S(1)}, bf16[1,512,512]{2,1,0:T(8,128)(2,1)}, u32[]{:S(2)}) copy-start(bf16[1,512,512]{2,1,0:T(8,128)(2,1)} %refs_8_.1) | copy-start | bytes 1572868
  15.3 0.9 %copy-start.6 = (bf16[4,64,512]{2,1,0:T(8,128)(2,1)S(1)}, bf16[4,64,512]{2,1,0:T(8,128)(2,1)}, u32[]{:S(2)}) copy-start(bf16[4,64,512]{2,1,0:T(8,128)(2,1)} %refs_9_.1) | copy-start | bytes 786436
  16.3 0.9 %copy-start.7 = (bf16[4,64,512]{2,1,0:T(8,128)(2,1)S(1)}, bf16[4,64,512]{2,1,0:T(8,128)(2,1)}, u32[]{:S(2)}) copy-start(bf16[4,64,512]{2,1,0:T(8,128)(2,1)} %refs_10_.1) | copy-start | bytes 786436
  17.2 0.8 %copy-start.8 = (bf16[4,4,1536]{2,1,0:T(4,128)(2,1)S(1)}, bf16[4,4,1536]{2,1,0:T(4,128)(2,1)}, u32[]{:S(2)}) copy-start(bf16[4,4,1536]{2,1,0:T(4,128)(2,1)} %refs_0_.1) | copy-start | bytes 147460
  18.0 0.7 %copy-start.9 = (f32[3072]{0:T(1024)S(1)}, f32[3072]{0:T(1024)}, u32[]{:S(2)}) copy-start(f32[3072]{0:T(1024)} %param.13) | copy-start | bytes 36868
  18.7 0.7 %copy-start.10 = (s32[4,64]{1,0:T(4,128)S(1)}, s32[4,64]{1,0:T(4,128)}, u32[]{:S(2)}) copy-start(s32[4,64]{1,0:T(4,128)} %parents_ref.1) | copy-start | bytes 3076
  19.4 0.7 %copy-start.11 = (s32[8]{0:T(128)S(1)}, s32[8]{0:T(128)}, u32[]{:S(2)}) copy-start(s32[8]{0:T(128)} %lengths_ref.1) | copy-start | bytes 100
  20.1 11.6 %copy-start = (bf16[1024,3072]{1,0:T(8,128)(2,1)S(1)}, bf16[1024,3072]{1,0:T(8,128)(2,1)}, u32[]{:S(2)}) copy-start(bf16[1024,3072]{1,0:T(8,128)(2,1)} %w_out.1) | copy-start | bytes 18874372
  27.5 4.1 %collective-permute-start.3 = (bf16[16,1408]{1,0:T(8,128)(2,1)S(1)}, bf16[16,1408]{1,0:T(8,128)(2,1)S(1)}, u32[]{:S(2)}, u32[]{:S(2)}) collective-permute-start(bf16[16,1408]{1,0:T(8,128)(2,1)S(1)} %get-tuple-element.12), channel_id=1, source_target_pairs={{0,2},{2,0},{4,6},{6,4},{8,10},{10,8},{12,14},{14,12},{16,18},{18,... | collective-permute-start | bytes 135176 | tf_op jit(solution)/shard_map/ppermute | solution.py:21
  34.2 1.3 %collective-permute-start.4 = (bf16[4,4,1536]{2,1,0:T(4,128)(2,1)S(1)}, bf16[4,4,1536]{2,1,0:T(4,128)(2,1)S(1)}, u32[]{:S(2)}, u32[]{:S(2)}) collective-permute-start(bf16[4,4,1536]{2,1,0:T(4,128)(2,1)S(1)} %get-tuple-element.14), channel_id=1, source_target_pairs={{0,1},{1,0},{2,3},{3,2},{4,5},{5,4},{6,7},{7,6},{8,9},{9,8},{10,11... | collective-permute-start | bytes 147464 | tf_op jit(solution)/shard_map/ppermute | solution.py:31

commit v2 on v1

v2 whole, which is shorter than its diff:
```python
import functools
import math

import jax
import jax.numpy as jnp
from jax import lax
from jax.experimental import pallas as pl
from jax.experimental.pallas import tpu as pltpu
from jax.sharding import PartitionSpec as P

HD = 128
BEAMS = 8

norm_eps = 1e-05
masked_score = -1e30
rope_base = 500000.0


def permute_by(value, axis, distance):
    pairs = [(source, source ^ distance) for source in range(lax.axis_size(axis))]
    return lax.ppermute(value, axis, pairs)


def across(value, beam_distance, tp_distance):
    req, tp = lax.axis_size("req"), lax.axis_size("tp")
    pairs = [
        (r * tp + t, (r ^ beam_distance) * tp + (t ^ tp_distance))
        for r in range(req)
        for t in range(tp)
    ]
    return lax.ppermute(value, ("req", "tp"), pairs)


def load_kernel(
    sizes,
    lengths,
    parents,
    gain,
    hidden,
    wq,
    wk,
    wv,
    pk,
    pv,
    gk,
    gv,
    gain_ref,
    x_ref,
    wq_ref,
    wk_ref,
    wv_ref,
    pk_ref,
    pv_ref,
    gk_ref,
    gv_ref,
    cosine_ref,
    sine_ref,
    prompt_bias_ref,
    gen_bias_ref,
    new_bias_ref,
    lengths_s,
    parents_s,
    hidden_s,
    sems,
):
    steps, own, group, half_len, history = sizes
    rows = steps * own
    device = lax.axis_index("req")
    request = device // 2
    parity = device % 2

    small = [
        pltpu.make_async_copy(source, target, sems.at[n])
        for n, (source, target) in enumerate(
            ((lengths, lengths_s), (parents, parents_s), (gain, gain_ref), (hidden, hidden_s))
        )
    ]
    large = []
    for source, target, parts in (
        (wq, wq_ref, 4),
        (wk, wk_ref, 2),
        (wv, wv_ref, 2),
    ):
        size = source.shape[0] // parts
        for n in range(parts):
            place = pl.ds(n * size, size)
            large.append((source.at[place], target.at[place]))
    large += [(pk, pk_ref), (pv, pv_ref), (gk, gk_ref), (gv, gv_ref)]
    large = [
        pltpu.make_async_copy(source, target, sems.at[len(small) + n])
        for n, (source, target) in enumerate(large)
    ]
    for copy in small + large:
        copy.start()
    for copy in small:
        copy.wait()

    for s in range(steps):
        x_ref[pl.ds(s * own, own), :] = hidden_s[s].astype(jnp.float32)

    length = lengths_s[request]
    row = lax.broadcasted_iota(jnp.int32, (2 * rows, HD), 0)
    lane = lax.broadcasted_iota(jnp.int32, (2 * rows, HD), 1)
    half_dim = HD // 2
    inverse = jnp.exp((lane % half_dim).astype(jnp.float32) * (-math.log(rope_base) / half_dim))
    step = (row % rows) // own
    angle = (length + history + step).astype(jnp.float32) * inverse
    sine = jnp.sin(angle)
    cosine_ref[...] = jnp.cos(angle)
    sine_ref[...] = jnp.where(lane < half_dim, -sine, sine)

    count = group * 2 * rows

    def parent_of(s, beam):
        out = jnp.zeros_like(beam)
        for j in range(BEAMS):
            out = jnp.where(beam == j, parents_s[s, request * BEAMS + j], out)
        return out

    row = lax.broadcasted_iota(jnp.int32, (count, HD), 0) % (2 * rows)
    row_step = (row % rows) // own
    row_parity = jnp.where(row < rows, parity, 1 - parity)
    beam = row_parity * own + row % own
    ancestors = [None] * steps
    at = beam
    for s in reversed(range(steps)):
        if s < steps - 1:
            at = jnp.where(row_step > s, parent_of(s + 1, at), beam)
        ancestors[s] = jnp.where(row_step >= s, at, -1)
    origin = parent_of(0, at)
    lane = lax.broadcasted_iota(jnp.int32, (count, HD), 1)

    for c in range(own * history // HD):
        key_beam = parity * own + (c * HD + lane) // history
        gen_bias_ref[:, pl.ds(c * HD, HD)] = jnp.where(key_beam == origin, 0.0, masked_score)
    new_bias = jnp.full((count, HD), masked_score, jnp.float32)
    for s in range(steps):
        hit = (lane // own == s) & (ancestors[s] == parity * own + lane % own)
        new_bias = jnp.where(hit, 0.0, new_bias)
    new_bias_ref[...] = new_bias
    place = parity * half_len + lax.broadcasted_iota(jnp.int32, prompt_bias_ref.shape, 1)
    prompt_bias_ref[...] = jnp.where(place < length, 0.0, masked_score)
    for copy in large:
        copy.wait()


def attend_kernel(
    sizes,
    gain_ref,
    x_ref,
    wq_ref,
    wk_ref,
    wv_ref,
    pk_ref,
    pv_ref,
    gk_ref,
    gv_ref,
    cosine_ref,
    sine_ref,
    prompt_bias_ref,
    gen_bias_ref,
    new_bias_ref,
    w_out,
    *refs,
):
    steps, own, tp, kv, group, history = sizes
    pieces = (None,) + refs[: 2 * tp - 1]
    kept_ref, kept_lse_ref, sent_ref, w_out_ref, x_s, xn_s, sems = refs[2 * tp - 1 :]
    rows = steps * own
    part = x_ref.shape[-1]
    width = part * tp
    heads = kv * group
    me_tp = lax.axis_index("tp")

    copies = [
        pltpu.make_async_copy(
            w_out.at[:, pl.ds(pl.multiple_of((me_tp ^ d) * part, HD), part)],
            w_out_ref.at[d],
            sems.at[d],
        )
        for d in range(tp)
    ]
    for copy in copies:
        copy.start()

    squares = []
    for b in range(2):
        total = jnp.zeros((rows, HD), jnp.float32)
        for t in range(tp):
            column = pl.multiple_of((me_tp ^ t) * part, HD)
            if (b, t) == (0, 0):
                mine = x_ref[...]
            else:
                for s in range(steps):
                    x_s[b * tp + t, pl.ds(s * own, own), :] = pieces[b * tp + t][s].astype(
                        jnp.float32
                    )
                mine = x_s[b * tp + t]
            xn_s[pl.ds(b * rows, rows), pl.ds(column, part)] = (
                mine * gain_ref[:, pl.ds(column, part)]
            ).astype(jnp.bfloat16)
            mine = mine * mine
            for c in range(part // HD):
                total = total + mine[:, c * HD : (c + 1) * HD]
        squares.append(jnp.sum(total, axis=-1, keepdims=True))
    scale = lax.rsqrt(jnp.concatenate(squares, axis=0) / width + norm_eps)
    cosine = cosine_ref[...] * scale
    sine = sine_ref[...] * scale

    def rotate(x):
        return x * cosine + pltpu.roll(x, HD // 2, 1) * sine

    def project(w_ref, lower, size):
        return jnp.dot(
            xn_s[...], w_ref[:, pl.ds(lower, size)], preferred_element_type=jnp.float32
        )

    def heads_of(w_ref, finish):
        size = math.gcd(w_ref.shape[1], 2 * HD)
        out = []
        for lower in range(0, w_ref.shape[1], size):
            block = project(w_ref, lower, size)
            for c in range(size // HD):
                out.append(finish(block[:, c * HD : (c + 1) * HD]).astype(jnp.bfloat16))
        return out

    queries = heads_of(wq_ref, rotate)
    new_keys = heads_of(wk_ref, rotate)
    new_values = heads_of(wv_ref, lambda x: x * scale)

    scaling = HD**-0.5
    contract = (((1,), (1,)), ((), ()))
    lane = lax.broadcasted_iota(jnp.int32, (rows, HD), 1)
    kept_lse = jnp.zeros((rows, HD), jnp.float32)
    sent_lse = jnp.zeros((rows, HD), jnp.float32)
    for g in range(kv):
        cols = pl.ds(g * HD, HD)
        q = jnp.concatenate(queries[g * group : (g + 1) * group], axis=0)
        keys = (
            pk_ref[0, :, cols],
            gk_ref[:, :, cols].reshape(own * history, HD),
            new_keys[g][:rows],
        )
        values = (
            pv_ref[0, :, cols],
            gv_ref[:, :, cols].reshape(own * history, HD),
            new_values[g][:rows],
        )
        biases = (prompt_bias_ref[...], gen_bias_ref[...], new_bias_ref[:, pl.ds(0, rows)])
        scores = [
            lax.dot_general(q, k, contract, preferred_element_type=jnp.float32) * scaling + bias
            for k, bias in zip(keys, biases)
        ]
        top = functools.reduce(
            jnp.maximum, [jnp.max(x, axis=-1, keepdims=True) for x in scores]
        )
        powers = [jnp.exp(x - top) for x in scores]
        total = sum(jnp.sum(x, axis=-1, keepdims=True) for x in powers)
        mixed = sum(
            jnp.dot(x.astype(jnp.bfloat16), v, preferred_element_type=jnp.float32)
            for x, v in zip(powers, values)
        )
        mixed = mixed / total
        lse = top + jnp.log(total)
        for j in range(group):
            h = g * group + j
            lower = j * 2 * rows
            kept_ref[:, pl.ds(h * HD, HD)] = mixed[lower : lower + rows]
            sent_ref[:, pl.ds(h * HD, HD)] = mixed[lower + rows : lower + 2 * rows].astype(
                jnp.bfloat16
            )
            kept_lse = jnp.where(lane == h, lse[lower : lower + rows], kept_lse)
            sent_lse = jnp.where(lane % heads == h, lse[lower + rows : lower + 2 * rows], sent_lse)
    kept_lse_ref[...] = kept_lse
    terms = jnp.zeros((rows, HD), jnp.float32)
    rest = sent_lse
    for n in range(3):
        term = rest.astype(jnp.bfloat16).astype(jnp.float32)
        terms = jnp.where(lane // heads == n, term, terms)
        rest = rest - term
    sent_ref[:, pl.ds(heads * HD, HD)] = terms.astype(jnp.bfloat16)
    for copy in copies:
        copy.wait()


def project_kernel(sizes, kept_ref, kept_lse_ref, got_ref, w_out_ref, *refs):
    steps, own, tp, heads, chunk = sizes
    outs = refs[:tp]
    (ctx_s,) = refs[tp:]
    part = outs[0].shape[-1]
    base = heads * HD
    lse_mine = kept_lse_ref[...]
    terms = got_ref[:, pl.ds(base, HD)].astype(jnp.float32)
    lse_got = terms + pltpu.roll(terms, HD - heads, 1) + pltpu.roll(terms, HD - 2 * heads, 1)
    top = jnp.maximum(lse_mine, lse_got)
    mine = jnp.exp(lse_mine - top)
    got = jnp.exp(lse_got - top)
    share = mine / (mine + got)
    for h in range(heads):
        cols = pl.ds(h * HD, HD)
        w = share[:, h : h + 1]
        ctx_s[:, cols] = (
            kept_ref[:, cols] * w + got_ref[:, cols].astype(jnp.float32) * (1.0 - w)
        ).astype(jnp.bfloat16)
    for d in list(range(1, tp)) + [0]:
        for lower in range(0, part, chunk):
            cols = pl.ds(lower, chunk)
            out = jnp.dot(ctx_s[...], w_out_ref[d, :, cols], preferred_element_type=jnp.float32)
            for s in range(steps):
                outs[d][s, :, cols] = out[s * own : (s + 1) * own].astype(outs[d].dtype)


def body(
    hidden_in,
    norm_gain,
    w_query,
    w_key,
    w_value,
    w_out,
    prompt_keys,
    prompt_values,
    gen_keys,
    gen_values,
    lengths,
    parents,
):
    steps, own, part = hidden_in.shape
    tp = lax.axis_size("tp")
    rows = steps * own
    width = w_query.shape[0]
    kv = w_key.shape[1] // HD
    group = w_query.shape[1] // w_key.shape[1]
    heads = kv * group
    half_len = prompt_keys.shape[1]
    history = gen_keys.shape[1]

    pieces = [
        across(hidden_in, b, t) for b in range(2) for t in range(tp) if (b, t) != (0, 0)
    ]

    def in_hbm(x):
        return pltpu.with_memory_space_constraint(x, pltpu.HBM)

    vmem = pl.BlockSpec(memory_space=pltpu.VMEM)
    hbm = pl.BlockSpec(memory_space=pltpu.HBM)
    params = pltpu.CompilerParams(vmem_limit_bytes=16 * 2**20)
    f32, bf16 = jnp.float32, jnp.bfloat16
    big = (w_query, w_key, w_value, prompt_keys, prompt_values, gen_keys, gen_values)
    loaded = pl.pallas_call(
        functools.partial(load_kernel, (steps, own, group, half_len, history)),
        out_shape=(
            jax.ShapeDtypeStruct((1, width), f32),
            jax.ShapeDtypeStruct((rows, part), f32),
            *(jax.ShapeDtypeStruct(x.shape, x.dtype) for x in big),
            jax.ShapeDtypeStruct((2 * rows, HD), f32),
            jax.ShapeDtypeStruct((2 * rows, HD), f32),
            jax.ShapeDtypeStruct((1, half_len), f32),
            jax.ShapeDtypeStruct((group * 2 * rows, own * history), f32),
            jax.ShapeDtypeStruct((group * 2 * rows, HD), f32),
        ),
        in_specs=[hbm] * 11,
        out_specs=(vmem,) * 14,
        scratch_shapes=[
            pltpu.SMEM(lengths.shape, jnp.int32),
            pltpu.SMEM(parents.shape, jnp.int32),
            pltpu.VMEM(hidden_in.shape, bf16),
            pltpu.SemaphoreType.DMA((16,)),
        ],
        compiler_params=params,
        name="load",
    )(*(in_hbm(x) for x in (lengths, parents, norm_gain[None, :], hidden_in, *big)))

    kept, kept_lse, sent, w_out_near = pl.pallas_call(
        functools.partial(attend_kernel, (steps, own, tp, kv, group, history)),
        out_shape=(
            jax.ShapeDtypeStruct((rows, heads * HD), f32),
            jax.ShapeDtypeStruct((rows, HD), f32),
            jax.ShapeDtypeStruct((rows, heads * HD + HD), bf16),
            jax.ShapeDtypeStruct((tp, heads * HD, part), bf16),
        ),
        in_specs=[vmem] * 14 + [hbm] + [vmem] * (2 * tp - 1),
        out_specs=(vmem,) * 4,
        scratch_shapes=[
            pltpu.VMEM((2 * tp, rows, part), f32),
            pltpu.VMEM((2 * rows, width), bf16),
            pltpu.SemaphoreType.DMA((tp,)),
        ],
        compiler_params=params,
        name="attend",
    )(*loaded, in_hbm(w_out), *pieces)

    got = permute_by(sent, "req", 1)

    out_types = [f32] + [bf16] * (tp - 1)
    sums = pl.pallas_call(
        functools.partial(project_kernel, (steps, own, tp, heads, math.gcd(part, 512))),
        out_shape=tuple(jax.ShapeDtypeStruct((steps, own, part), kind) for kind in out_types),
        in_specs=[vmem] * 4,
        out_specs=(vmem,) * tp,
        scratch_shapes=[pltpu.VMEM((rows, heads * HD), bf16)],
        compiler_params=params,
        name="project",
    )(kept, kept_lse, got, w_out_near)
    total = sums[0]
    for t in range(1, tp):
        total = total + across(sums[t], 0, t).astype(f32)
    return total.astype(bf16)


def solution(mesh):
    in_specs = (
        P(None, "req", "tp"),
        P(),
        P(None, "tp"),
        P(None, "tp"),
        P(None, "tp"),
        P("tp", None),
        P("req", None, "tp"),
        P("req", None, "tp"),
        P("req", None, "tp"),
        P("req", None, "tp"),
        P(),
        P(),
    )
    out_specs = P(None, "req", "tp")
    return jax.shard_map(body, mesh=mesh, in_specs=in_specs, out_specs=out_specs, check_vma=False)
```

time: 36.7 us -> 21.8 us (0.59); the launches traced: 36.1 us -> 21.7 us
  local copies, waits for them, and re-layouts: 13.4 us -> 0 us
  waiting for transfers between devices: 7.87 us -> 3.18 us
  Pallas kernels: 9.98 us -> 12.7 us
  starting transfers between devices: 4.13 us -> 5.15 us
    unnamed x24 -> x0, local copies, waits for them, and re-layouts: 13.4 us -> none
    pallas_call x1 -> x2, Pallas kernels: 7.44 us -> 11.6 us  [the longest x1 6.4 us: body(): pl.pallas_call(functools.partial(attend_kernel, (steps, own, tp, kv, grou...]
    ppermute x4, waiting for transfers between devices: 4.74 us -> 1.24 us  [across(): return lax.ppermute(value, ('req', 'tp'), pairs)]
    pallas_call x1, Pallas kernels: 2.54 us -> 1.09 us  [body(): pl.pallas_call(functools.partial(project_kernel, (steps, own, tp, heads,...]
    ppermute x1, waiting for transfers between devices: 3.14 us -> 1.94 us  [permute_by(): return lax.ppermute(value, axis, pairs)]
    ppermute x1, starting transfers between devices: 1 us -> 2.09 us  [permute_by(): return lax.ppermute(value, axis, pairs)]
  transfers between devices with their start and end apart: 5 -> 5, of which waited for: 4 -> 2; matrix products, arithmetic and copies ran while one was open for 0% -> 0% of each run, Pallas kernels for 0% -> 24%
where the time goes in v2:
time: 21.8 us; the launch traced here: 21.7 us
  Pallas kernels  12.7 us (58%)
  starting transfers between devices  5.15 us (24%)
  waiting for transfers between devices  3.18 us (15%)
  other arithmetic  0.65 us (3%)
    pallas_call x1, Pallas kernels, body(): pl.pallas_call(functools.partial(attend_kernel, (steps, own, tp, kv, grou...  6.4 us
    pallas_call x1, Pallas kernels, body(): pl.pallas_call(functools.partial(load_kernel, (steps, own, group, half_le...  5.17 us
    ppermute x4, starting transfers between devices, across(): return lax.ppermute(value, ('req', 'tp'), pairs)  3.06 us
    ppermute x1, starting transfers between devices, permute_by(): return lax.ppermute(value, axis, pairs)  2.09 us
    ppermute x1, waiting for transfers between devices, permute_by(): return lax.ppermute(value, axis, pairs)  1.94 us
    ppermute x4, waiting for transfers between devices, across(): return lax.ppermute(value, ('req', 'tp'), pairs)  1.24 us
    pallas_call x1, Pallas kernels, body(): pl.pallas_call(functools.partial(project_kernel, (steps, own, tp, heads,...  1.09 us
    convert_element_type x1, other arithmetic, body(): return total.astype(bf16)  0.65 us
  transfers between devices with their start and end apart: 5, of which 2 were waited for; matrix products, arithmetic and copies ran while one was open for 0% of the time, Pallas kernels for 24%

profile of v2, /device:TPU:0, one launch (start us, length us, event | category | flops | bytes accessed | tf_op | source)
XLA Modules:
  0.0 21.7 jit_solution(7347119961675219328)
XLA Ops:
  0.0 0.5 %collective-permute-start = (bf16[4,4,1536]{2,1,0:T(4,128)(2,1)}, bf16[4,4,1536]{2,1,0:T(4,128)(2,1)S(1)}, u32[]{:S(2)}, u32[]{:S(2)}) collective-permute-start(bf16[4,4,1536]{2,1,0:T(4,128)(2,1)} %hidden.1), channel_id=1, source_target_pairs={{0,1},{1,0},{2,3},{3,2},{4,5},{5,4},{6,7},{7,6},{8,9},{9,8},{10,11... | collective-permute-start | bytes 147464 | tf_op jit(solution)/shard_map/ppermute | solution.py:31
  0.5 2.6 %collective-permute-start.2 = (bf16[4,4,1536]{2,1,0:T(4,128)(2,1)}, bf16[4,4,1536]{2,1,0:T(4,128)(2,1)S(1)}, u32[]{:S(2)}, u32[]{:S(2)}) collective-permute-start(bf16[4,4,1536]{2,1,0:T(4,128)(2,1)} %hidden.1), channel_id=1, source_target_pairs={{0,3},{1,2},{2,1},{3,0},{4,7},{5,6},{6,5},{7,4},{8,11},{9,10},{10,... | collective-permute-start | bytes 147464 | tf_op jit(solution)/shard_map/ppermute | solution.py:31
  3.1 0.0 collective-permute-start.1
  3.1 5.2 %load.1 = (f32[1,3072]{1,0:T(1,128)S(1)}, f32[16,1536]{1,0:T(8,128)S(1)}, bf16[3072,1024]{1,0:T(8,128)(2,1)S(1)}, bf16[3072,512]{1,0:T(8,128)(2,1)S(1)}, bf16[30...) custom-call(s32[8]{0:T(128)} %lengths.1, ...), custom_call_target="tpu_custom_call" | custom-call | tf_op jit(solution)/shard_map/load/pallas_call | solution.py:349
  8.2 0.0 collective-permute-done.refs_0_
  8.2 0.0 collective-permute-done.2.refs_2_
  8.3 0.0 collective-permute-done.1.refs_1_
  8.3 6.4 %attend.1 = (f32[16,1024]{1,0:T(8,128)S(1)}, f32[16,128]{1,0:T(8,128)S(1)}, bf16[16,1152]{1,0:T(8,128)(2,1)S(1)}, bf16[2,1024,1536]{2,1,0:T(8,128)(2,1)S(1)}) custom-call(f32[1,3072]{1,0:T(1,128)S(1)} %get-tuple-element.25.gain_ref, f32[16,1536]{1,0:T(8,128)S(1)} %get-tuple-element.26.x_ref, bf16[3072,1024]{1,0:T(8,128)(2,1)S(1)} %get-tuple-element.27.wq_ref, ...), custom_call_target="tpu_custom_call" | custom-call | tf_op jit(solution)/shard_map/attend/pallas_call | solution.py:373
  14.7 2.1 %collective-permute-start.3 = (bf16[16,1152]{1,0:T(8,128)(2,1)S(1)}, bf16[16,1152]{1,0:T(8,128)(2,1)S(1)}, u32[]{:S(2)}, u32[]{:S(2)}) collective-permute-start(bf16[16,1152]{1,0:T(8,128)(2,1)S(1)} %get-tuple-element.41), channel_id=1, source_target_pairs={{0,2},{2,0},{4,6},{6,4},{8,10},{10,8},{12,14},{14,12},{16,18},{18,... | collective-permute-start | bytes 110600 | tf_op jit(solution)/shard_map/ppermute | solution.py:21
  16.8 1.9 %collective-permute-done.3.got_ref = bf16[16,1152]{1,0:T(8,128)(2,1)S(1)} collective-permute-done((bf16[16,1152]{1,0:T(8,128)(2,1)S(1)}, bf16[16,1152]{1,0:T(8,128)(2,1)S(1)}, u32[]{:S(2)}, u32[]{:S(2)}) %collective-permute-start.3) | collective-permute-done | bytes 36896 | tf_op jit(solution)/shard_map/ppermute | solution.py:21
  18.7 1.1 %project.1 = (f32[4,4,1536]{2,1,0:T(4,128)S(1)}, bf16[4,4,1536]{2,1,0:T(4,128)(2,1)S(1)}) custom-call(f32[16,1024]{1,0:T(8,128)S(1)} %get-tuple-element.39.kept_ref, f32[16,128]{1,0:T(8,128)S(1)} %get-tuple-element.40.kept_lse_ref, bf16[16,1152]{1,0:T(8,128)(2,1)S(1)} %collective-permute-done.3.got_ref, bf16[2,1024,1536]{2,1,0:T(8,128)(2,1)S(1)} %get-tuple-element.42.w_out_ref), custom_call_target="tpu_custom_call" | custom-call | tf_op jit(solution)/shard_map/project/pallas_call | solution.py:395
  19.8 0.0 collective-permute-start.4
  19.8 1.2 %collective-permute-done.4 = bf16[4,4,1536]{2,1,0:T(4,128)(2,1)S(1)} collective-permute-done((bf16[4,4,1536]{2,1,0:T(4,128)(2,1)S(1)}, bf16[4,4,1536]{2,1,0:T(4,128)(2,1)S(1)}, u32[]{:S(2)}, u32[]{:S(2)}) %collective-permute-start.4) | collective-permute-done | bytes 49184 | tf_op jit(solution)/shard_map/ppermute | solution.py:31
  21.0 0.6 %add_convert_fusion = bf16[4,4,1536]{2,1,0:T(4,128)(2,1)} fusion(f32[4,4,1536]{2,1,0:T(4,128)S(1)} %get-tuple-element.43, bf16[4,4,1536]{2,1,0:T(4,128)(2,1)S(1)} %collective-permute-done.4), kind=kLoop, calls=%fused_computation | loop fusion | flops 73728 | bytes 196608 | tf_op jit(solution)/shard_map/convert_element_type | solution.py:407
Async XLA Ops:
  0.0 8.2 %collective-permute-start = (bf16[4,4,1536]{2,1,0:T(4,128)(2,1)}, bf16[4,4,1536]{2,1,0:T(4,128)(2,1)S(1)}, u32[]{:S(2)}, u32[]{:S(2)}) collective-permute-start(bf16[4,4,1536]{2,1,0:T(4,128)(2,1)} %hidden.1), channel_id=1, source_target_pairs={{0,1},{1,0},{2,3},{3,2},{4,5},{5,4},{6,7},{7,6},{8,9},{9,8},{10,11... | collective-permute-start | bytes 147464 | tf_op jit(solution)/shard_map/ppermute | solution.py:31
  0.5 7.8 %collective-permute-start.2 = (bf16[4,4,1536]{2,1,0:T(4,128)(2,1)}, bf16[4,4,1536]{2,1,0:T(4,128)(2,1)S(1)}, u32[]{:S(2)}, u32[]{:S(2)}) collective-permute-start(bf16[4,4,1536]{2,1,0:T(4,128)(2,1)} %hidden.1), channel_id=1, source_target_pairs={{0,3},{1,2},{2,1},{3,0},{4,7},{5,6},{6,5},{7,4},{8,11},{9,10},{10,... | collective-permute-start | bytes 147464 | tf_op jit(solution)/shard_map/ppermute | solution.py:31
  3.1 5.2 %collective-permute-start.1 = (bf16[4,4,1536]{2,1,0:T(4,128)(2,1)}, bf16[4,4,1536]{2,1,0:T(4,128)(2,1)S(1)}, u32[]{:S(2)}, u32[]{:S(2)}) collective-permute-start(bf16[4,4,1536]{2,1,0:T(4,128)(2,1)} %hidden.1), channel_id=1, source_target_pairs={{0,2},{1,3},{2,0},{3,1},{4,6},{5,7},{6,4},{7,5},{8,10},{9,11},{10,... | collective-permute-start | bytes 147464 | tf_op jit(solution)/shard_map/ppermute | solution.py:31
  14.7 4.0 %collective-permute-start.3 = (bf16[16,1152]{1,0:T(8,128)(2,1)S(1)}, bf16[16,1152]{1,0:T(8,128)(2,1)S(1)}, u32[]{:S(2)}, u32[]{:S(2)}) collective-permute-start(bf16[16,1152]{1,0:T(8,128)(2,1)S(1)} %get-tuple-element.41), channel_id=1, source_target_pairs={{0,2},{2,0},{4,6},{6,4},{8,10},{10,8},{12,14},{14,12},{16,18},{18,... | collective-permute-start | bytes 110600 | tf_op jit(solution)/shard_map/ppermute | solution.py:21
  19.8 1.2 %collective-permute-start.4 = (bf16[4,4,1536]{2,1,0:T(4,128)(2,1)S(1)}, bf16[4,4,1536]{2,1,0:T(4,128)(2,1)S(1)}, u32[]{:S(2)}, u32[]{:S(2)}) collective-permute-start(bf16[4,4,1536]{2,1,0:T(4,128)(2,1)S(1)} %get-tuple-element.44), channel_id=1, source_target_pairs={{0,1},{1,0},{2,3},{3,2},{4,5},{5,4},{6,7},{7,6},{8,9},{9,8},{10,11... | collective-permute-start | bytes 147464 | tf_op jit(solution)/shard_map/ppermute | solution.py:31

commit v3 on v2

--- a/solution.py
+++ b/solution.py
@@ -39,7 +39,6 @@
     hidden,
     wq,
     wk,
-    wv,
     pk,
     pv,
     gk,
@@ -48,51 +47,50 @@
     x_ref,
     wq_ref,
     wk_ref,
-    wv_ref,
-    pk_ref,
-    pv_ref,
-    gk_ref,
-    gv_ref,
+    keys_ref,
+    values_ref,
     cosine_ref,
     sine_ref,
-    prompt_bias_ref,
-    gen_bias_ref,
-    new_bias_ref,
+    bias_ref,
     lengths_s,
     parents_s,
     hidden_s,
     sems,
 ):
-    steps, own, group, half_len, history = sizes
+    steps, own, kv, group, history = sizes
     rows = steps * own
+    blocks = pk.shape[0]
+    half_len = blocks * history
     device = lax.axis_index("req")
     request = device // 2
     parity = device % 2
 
     small = [
-        pltpu.make_async_copy(source, target, sems.at[n])
-        for n, (source, target) in enumerate(
-            ((lengths, lengths_s), (parents, parents_s), (gain, gain_ref), (hidden, hidden_s))
-        )
+        (lengths, lengths_s),
+        (parents, parents_s),
+        (gain, gain_ref),
+        (hidden, hidden_s),
     ]
     large = []
-    for source, target, parts in (
-        (wq, wq_ref, 4),
-        (wk, wk_ref, 2),
-        (wv, wv_ref, 2),
-    ):
+    for g in range(kv):
+        cols = pl.ds(g * HD, HD)
+        for prompt, gen, target in ((pk, gk, keys_ref), (pv, gv, values_ref)):
+            large.append((prompt.at[:, :, cols], target.at[g, pl.ds(0, blocks), :, pl.ds(0, HD)]))
+            large.append((gen.at[:, :, cols], target.at[g, pl.ds(blocks, own), :, pl.ds(0, HD)]))
+    for source, target, parts in ((wk, wk_ref, 4), (wq, wq_ref, 8)):
         size = source.shape[0] // parts
         for n in range(parts):
             place = pl.ds(n * size, size)
             large.append((source.at[place], target.at[place]))
-    large += [(pk, pk_ref), (pv, pv_ref), (gk, gk_ref), (gv, gv_ref)]
-    large = [
-        pltpu.make_async_copy(source, target, sems.at[len(small) + n])
-        for n, (source, target) in enumerate(large)
-    ]
-    for copy in small + large:
+    copies = [
+        pltpu.make_async_copy(source, target, sems.at[n])
+        for n, (source, target) in enumerate(small + large)
+    ]
+    for copy in copies:
         copy.start()
-    for copy in small:
+    for g in range(kv):
+        values_ref[g, :, :, pl.ds(HD, HD)] = jnp.ones((blocks + own, history, HD), jnp.bfloat16)
+    for copy in copies[: len(small)]:
         copy.wait()
 
     for s in range(steps):
@@ -130,17 +128,20 @@
     origin = parent_of(0, at)
     lane = lax.broadcasted_iota(jnp.int32, (count, HD), 1)
 
+    for c in range(half_len // HD):
+        place = parity * half_len + c * HD + lane
+        bias_ref[:, pl.ds(c * HD, HD)] = jnp.where(place < length, 0.0, masked_score)
     for c in range(own * history // HD):
         key_beam = parity * own + (c * HD + lane) // history
-        gen_bias_ref[:, pl.ds(c * HD, HD)] = jnp.where(key_beam == origin, 0.0, masked_score)
+        bias_ref[:, pl.ds(half_len + c * HD, HD)] = jnp.where(
+            key_beam == origin, 0.0, masked_score
+        )
     new_bias = jnp.full((count, HD), masked_score, jnp.float32)
     for s in range(steps):
         hit = (lane // own == s) & (ancestors[s] == parity * own + lane % own)
         new_bias = jnp.where(hit, 0.0, new_bias)
-    new_bias_ref[...] = new_bias
-    place = parity * half_len + lax.broadcasted_iota(jnp.int32, prompt_bias_ref.shape, 1)
-    prompt_bias_ref[...] = jnp.where(place < length, 0.0, masked_score)
-    for copy in large:
+    bias_ref[:, pl.ds(half_len + own * history, HD)] = new_bias
+    for copy in copies[len(small) :]:
         copy.wait()
 
 
@@ -150,29 +151,27 @@
     x_ref,
     wq_ref,
     wk_ref,
-    wv_ref,
-    pk_ref,
-    pv_ref,
-    gk_ref,
-    gv_ref,
+    keys_ref,
+    values_ref,
     cosine_ref,
     sine_ref,
-    prompt_bias_ref,
-    gen_bias_ref,
-    new_bias_ref,
+    bias_ref,
+    wv,
     w_out,
     *refs,
 ):
-    steps, own, tp, kv, group, history = sizes
+    steps, own, tp, kv, group = sizes
     pieces = (None,) + refs[: 2 * tp - 1]
-    kept_ref, kept_lse_ref, sent_ref, w_out_ref, x_s, xn_s, sems = refs[2 * tp - 1 :]
+    kept_ref, kept_lse_ref, sent_ref, w_out_ref, x_s, xn_s, wv_s, sems = refs[2 * tp - 1 :]
     rows = steps * own
     part = x_ref.shape[-1]
     width = part * tp
     heads = kv * group
+    old = keys_ref.shape[1] * keys_ref.shape[2]
     me_tp = lax.axis_index("tp")
 
-    copies = [
+    copies = [pltpu.make_async_copy(wv, wv_s, sems.at[tp])]
+    copies += [
         pltpu.make_async_copy(
             w_out.at[:, pl.ds(pl.multiple_of((me_tp ^ d) * part, HD), part)],
             w_out_ref.at[d],
@@ -204,63 +203,76 @@
                 total = total + mine[:, c * HD : (c + 1) * HD]
         squares.append(jnp.sum(total, axis=-1, keepdims=True))
     scale = lax.rsqrt(jnp.concatenate(squares, axis=0) / width + norm_eps)
-    cosine = cosine_ref[...] * scale
-    sine = sine_ref[...] * scale
-
-    def rotate(x):
-        return x * cosine + pltpu.roll(x, HD // 2, 1) * sine
+    key_tables = (cosine_ref[...] * scale, sine_ref[...] * scale)
+    query_tables = tuple(x * HD**-0.5 for x in key_tables)
+
+    def rotate(x, tables):
+        return (x * tables[0] + pltpu.roll(x, HD // 2, 1) * tables[1]).astype(jnp.bfloat16)
 
     def project(w_ref, lower, size):
-        return jnp.dot(
+        block = jnp.dot(
             xn_s[...], w_ref[:, pl.ds(lower, size)], preferred_element_type=jnp.float32
         )
-
-    def heads_of(w_ref, finish):
+        return [block[:, c * HD : (c + 1) * HD] for c in range(size // HD)]
+
+    def project_all(w_ref):
         size = math.gcd(w_ref.shape[1], 2 * HD)
-        out = []
-        for lower in range(0, w_ref.shape[1], size):
-            block = project(w_ref, lower, size)
-            for c in range(size // HD):
-                out.append(finish(block[:, c * HD : (c + 1) * HD]).astype(jnp.bfloat16))
-        return out
-
-    queries = heads_of(wq_ref, rotate)
-    new_keys = heads_of(wk_ref, rotate)
-    new_values = heads_of(wv_ref, lambda x: x * scale)
-
-    scaling = HD**-0.5
+        return [x for c in range(0, w_ref.shape[1], size) for x in project(w_ref, c, size)]
+
+    pad = jnp.zeros((HD - rows, HD), jnp.bfloat16)
+    ones = jnp.ones((HD, HD), jnp.bfloat16)
     contract = (((1,), (1,)), ((), ()))
+    new_keys = [
+        jnp.concatenate([rotate(x, key_tables)[:rows], pad], axis=0) for x in project_all(wk_ref)
+    ]
+
+    def score(g):
+        q = jnp.concatenate(
+            [rotate(x, query_tables) for x in project(wq_ref, g * group * HD, group * HD)], axis=0
+        )
+        before = lax.dot_general(
+            q, keys_ref[g].reshape(old, HD), contract, preferred_element_type=jnp.float32
+        )
+        now = lax.dot_general(q, new_keys[g], contract, preferred_element_type=jnp.float32)
+        return before + bias_ref[:, pl.ds(0, old)], now + bias_ref[:, pl.ds(old, HD)]
+
+    def soften(before, now):
+        most = now
+        for c in range(old // HD):
+            most = jnp.maximum(most, before[:, c * HD : (c + 1) * HD])
+        top = jnp.max(most, axis=-1, keepdims=True)
+        return (
+            jnp.exp(before - top).astype(jnp.bfloat16),
+            jnp.exp(now - top).astype(jnp.bfloat16),
+            top,
+        )
+
+    scores, soft = [], []
+    for g in range(kv):
+        scores.append(score(g))
+        if g > 0:
+            soft.append(soften(*scores[g - 1]))
+    soft.append(soften(*scores[kv - 1]))
+
+    copies[0].wait()
+    new_values = [
+        jnp.concatenate([(x * scale).astype(jnp.bfloat16)[:rows], pad], axis=0)
+        for x in project_all(wv_s)
+    ]
     lane = lax.broadcasted_iota(jnp.int32, (rows, HD), 1)
     kept_lse = jnp.zeros((rows, HD), jnp.float32)
     sent_lse = jnp.zeros((rows, HD), jnp.float32)
     for g in range(kv):
-        cols = pl.ds(g * HD, HD)
-        q = jnp.concatenate(queries[g * group : (g + 1) * group], axis=0)
-        keys = (
-            pk_ref[0, :, cols],
-            gk_ref[:, :, cols].reshape(own * history, HD),
-            new_keys[g][:rows],
-        )
-        values = (
-            pv_ref[0, :, cols],
-            gv_ref[:, :, cols].reshape(own * history, HD),
-            new_values[g][:rows],
-        )
-        biases = (prompt_bias_ref[...], gen_bias_ref[...], new_bias_ref[:, pl.ds(0, rows)])
-        scores = [
-            lax.dot_general(q, k, contract, preferred_element_type=jnp.float32) * scaling + bias
-            for k, bias in zip(keys, biases)
-        ]
-        top = functools.reduce(
-            jnp.maximum, [jnp.max(x, axis=-1, keepdims=True) for x in scores]
-        )
-        powers = [jnp.exp(x - top) for x in scores]
-        total = sum(jnp.sum(x, axis=-1, keepdims=True) for x in powers)
-        mixed = sum(
-            jnp.dot(x.astype(jnp.bfloat16), v, preferred_element_type=jnp.float32)
-            for x, v in zip(powers, values)
-        )
-        mixed = mixed / total
+        before, now, top = soft[g]
+        mixed = jnp.dot(
+            before, values_ref[g].reshape(old, 2 * HD), preferred_element_type=jnp.float32
+        ) + jnp.dot(
+            now,
+            jnp.concatenate([new_values[g], ones], axis=1),
+            preferred_element_type=jnp.float32,
+        )
+        total = mixed[:, HD:]
+        mixed = mixed[:, :HD] / total
         lse = top + jnp.log(total)
         for j in range(group):
             h = g * group + j
@@ -279,7 +291,7 @@
         terms = jnp.where(lane // heads == n, term, terms)
         rest = rest - term
     sent_ref[:, pl.ds(heads * HD, HD)] = terms.astype(jnp.bfloat16)
-    for copy in copies:
+    for copy in copies[1:]:
         copy.wait()
 
 
@@ -331,7 +343,6 @@
     kv = w_key.shape[1] // HD
     group = w_query.shape[1] // w_key.shape[1]
     heads = kv * group
-    half_len = prompt_keys.shape[1]
     history = gen_keys.shape[1]
 
     pieces = [
@@ -345,49 +356,68 @@
     hbm = pl.BlockSpec(memory_space=pltpu.HBM)
     params = pltpu.CompilerParams(vmem_limit_bytes=16 * 2**20)
     f32, bf16 = jnp.float32, jnp.bfloat16
-    big = (w_query, w_key, w_value, prompt_keys, prompt_values, gen_keys, gen_values)
+    blocks = prompt_keys.shape[1] // history
+    old = (kv, blocks + own, history)
     loaded = pl.pallas_call(
-        functools.partial(load_kernel, (steps, own, group, half_len, history)),
+        functools.partial(load_kernel, (steps, own, kv, group, history)),
         out_shape=(
             jax.ShapeDtypeStruct((1, width), f32),
             jax.ShapeDtypeStruct((rows, part), f32),
-            *(jax.ShapeDtypeStruct(x.shape, x.dtype) for x in big),
+            jax.ShapeDtypeStruct(w_query.shape, bf16),
+            jax.ShapeDtypeStruct(w_key.shape, bf16),
+            jax.ShapeDtypeStruct((*old, HD), bf16),
+            jax.ShapeDtypeStruct((*old, 2 * HD), bf16),
             jax.ShapeDtypeStruct((2 * rows, HD), f32),
             jax.ShapeDtypeStruct((2 * rows, HD), f32),
-            jax.ShapeDtypeStruct((1, half_len), f32),
-            jax.ShapeDtypeStruct((group * 2 * rows, own * history), f32),
-            jax.ShapeDtypeStruct((group * 2 * rows, HD), f32),
+            jax.ShapeDtypeStruct((group * 2 * rows, (blocks + own) * history + HD), f32),
         ),
-        in_specs=[hbm] * 11,
-        out_specs=(vmem,) * 14,
+        in_specs=[hbm] * 10,
+        out_specs=(vmem,) * 9,
         scratch_shapes=[
             pltpu.SMEM(lengths.shape, jnp.int32),
             pltpu.SMEM(parents.shape, jnp.int32),
             pltpu.VMEM(hidden_in.shape, bf16),
-            pltpu.SemaphoreType.DMA((16,)),
+            pltpu.SemaphoreType.DMA((16 + 4 * kv,)),
         ],
         compiler_params=params,
         name="load",
-    )(*(in_hbm(x) for x in (lengths, parents, norm_gain[None, :], hidden_in, *big)))
+    )(
+        *(
+            in_hbm(x)
+            for x in (
+                lengths,
+                parents,
+                norm_gain[None, :],
+                hidden_in,
+                w_query,
+                w_key,
+                prompt_keys.reshape(blocks, history, kv * HD),
+                prompt_values.reshape(blocks, history, kv * HD),
+                gen_keys,
+                gen_values,
+            )
+        )
+    )
 
     kept, kept_lse, sent, w_out_near = pl.pallas_call(
-        functools.partial(attend_kernel, (steps, own, tp, kv, group, history)),
+        functools.partial(attend_kernel, (steps, own, tp, kv, group)),
         out_shape=(
             jax.ShapeDtypeStruct((rows, heads * HD), f32),
             jax.ShapeDtypeStruct((rows, HD), f32),
             jax.ShapeDtypeStruct((rows, heads * HD + HD), bf16),
             jax.ShapeDtypeStruct((tp, heads * HD, part), bf16),
         ),
-        in_specs=[vmem] * 14 + [hbm] + [vmem] * (2 * tp - 1),
+        in_specs=[vmem] * 9 + [hbm] * 2 + [vmem] * (2 * tp - 1),
         out_specs=(vmem,) * 4,
         scratch_shapes=[
             pltpu.VMEM((2 * tp, rows, part), f32),
             pltpu.VMEM((2 * rows, width), bf16),
-            pltpu.SemaphoreType.DMA((tp,)),
+            pltpu.VMEM(w_value.shape, bf16),
+            pltpu.SemaphoreType.DMA((tp + 1,)),
         ],
         compiler_params=params,
         name="attend",
-    )(*loaded, in_hbm(w_out), *pieces)
+    )(*loaded, in_hbm(w_value), in_hbm(w_out), *pieces)
 
     got = permute_by(sent, "req", 1)
 

time: 21.8 us -> 19.5 us (0.89)
  Pallas kernels: 12.7 us -> 10.4 us
    pallas_call x1, Pallas kernels: 6.4 us -> 4.66 us  [body(): pl.pallas_call(functools.partial(attend_kernel, (steps, own, tp, kv, grou...]
    pallas_call x1, Pallas kernels: 5.17 us -> 4.64 us  [body(): pl.pallas_call(functools.partial(load_kernel, (steps, own, kv, group, his...]
where the time goes in v3:
time: 19.5 us; the launch traced here: 19.4 us
  Pallas kernels  10.4 us (53%)
  starting transfers between devices  5.14 us (26%)
  waiting for transfers between devices  3.18 us (16%)
  other arithmetic  0.65 us (3%)
    pallas_call x1, Pallas kernels, body(): pl.pallas_call(functools.partial(attend_kernel, (steps, own, tp, kv, grou...  4.66 us
    pallas_call x1, Pallas kernels, body(): pl.pallas_call(functools.partial(load_kernel, (steps, own, kv, group, his...  4.64 us
    ppermute x4, starting transfers between devices, across(): return lax.ppermute(value, ('req', 'tp'), pairs)  3.06 us
    ppermute x1, starting transfers between devices, permute_by(): return lax.ppermute(value, axis, pairs)  2.08 us
    ppermute x1, waiting for transfers between devices, permute_by(): return lax.ppermute(value, axis, pairs)  1.94 us
    ppermute x4, waiting for transfers between devices, across(): return lax.ppermute(value, ('req', 'tp'), pairs)  1.24 us
    pallas_call x1, Pallas kernels, body(): pl.pallas_call(functools.partial(project_kernel, (steps, own, tp, heads,...  1.08 us
    convert_element_type x1, other arithmetic, body(): return total.astype(bf16)  0.65 us
  transfers between devices with their start and end apart: 5, of which 2 were waited for; matrix products, arithmetic and copies ran while one was open for 0% of the time, Pallas kernels for 24%

profile of v3, /device:TPU:0, one launch (start us, length us, event | category | flops | bytes accessed | tf_op | source)
XLA Modules:
  0.0 19.4 jit_solution(6517376713278798751)
XLA Ops:
  0.0 0.5 %collective-permute-start = (bf16[4,4,1536]{2,1,0:T(4,128)(2,1)}, bf16[4,4,1536]{2,1,0:T(4,128)(2,1)S(1)}, u32[]{:S(2)}, u32[]{:S(2)}) collective-permute-start(bf16[4,4,1536]{2,1,0:T(4,128)(2,1)} %hidden.1), channel_id=1, source_target_pairs={{0,1},{1,0},{2,3},{3,2},{4,5},{5,4},{6,7},{7,6},{8,9},{9,8},{10,11... | collective-permute-start | bytes 147464 | tf_op jit(solution)/shard_map/ppermute | solution.py:31
  0.5 2.6 %collective-permute-start.2 = (bf16[4,4,1536]{2,1,0:T(4,128)(2,1)}, bf16[4,4,1536]{2,1,0:T(4,128)(2,1)S(1)}, u32[]{:S(2)}, u32[]{:S(2)}) collective-permute-start(bf16[4,4,1536]{2,1,0:T(4,128)(2,1)} %hidden.1), channel_id=1, source_target_pairs={{0,3},{1,2},{2,1},{3,0},{4,7},{5,6},{6,5},{7,4},{8,11},{9,10},{10,... | collective-permute-start | bytes 147464 | tf_op jit(solution)/shard_map/ppermute | solution.py:31
  3.1 0.0 collective-permute-start.1
  3.1 4.6 %load.1 = (f32[1,3072]{1,0:T(1,128)S(1)}, f32[16,1536]{1,0:T(8,128)S(1)}, bf16[3072,1024]{1,0:T(8,128)(2,1)S(1)}, bf16[3072,512]{1,0:T(8,128)(2,1)S(1)}, bf16[4,...) custom-call(s32[8]{0:T(128)} %lengths.1, ...), custom_call_target="tpu_custom_call" | custom-call | tf_op jit(solution)/shard_map/load/pallas_call | solution.py:361
  7.7 0.0 collective-permute-done.refs_0_
  7.7 0.0 collective-permute-done.2.refs_2_
  7.7 0.0 collective-permute-done.1.refs_1_
  7.7 4.7 %attend.1 = (f32[16,1024]{1,0:T(8,128)S(1)}, f32[16,128]{1,0:T(8,128)S(1)}, bf16[16,1152]{1,0:T(8,128)(2,1)S(1)}, bf16[2,1024,1536]{2,1,0:T(8,128)(2,1)S(1)}) custom-call(f32[1,3072]{1,0:T(1,128)S(1)} %get-tuple-element.20.gain_ref, f32[16,1536]{1,0:T(8,128)S(1)} %get-tuple-element.21.x_ref, bf16[3072,1024]{1,0:T(8,128)(2,1)S(1)} %get-tuple-element.22.wq_ref, ...), custom_call_target="tpu_custom_call" | custom-call | tf_op jit(solution)/shard_map/attend/pallas_call | solution.py:402
  12.4 2.1 %collective-permute-start.3 = (bf16[16,1152]{1,0:T(8,128)(2,1)S(1)}, bf16[16,1152]{1,0:T(8,128)(2,1)S(1)}, u32[]{:S(2)}, u32[]{:S(2)}) collective-permute-start(bf16[16,1152]{1,0:T(8,128)(2,1)S(1)} %get-tuple-element.31), channel_id=1, source_target_pairs={{0,2},{2,0},{4,6},{6,4},{8,10},{10,8},{12,14},{14,12},{16,18},{18,... | collective-permute-start | bytes 110600 | tf_op jit(solution)/shard_map/ppermute | solution.py:21
  14.5 1.9 %collective-permute-done.3.got_ref = bf16[16,1152]{1,0:T(8,128)(2,1)S(1)} collective-permute-done((bf16[16,1152]{1,0:T(8,128)(2,1)S(1)}, bf16[16,1152]{1,0:T(8,128)(2,1)S(1)}, u32[]{:S(2)}, u32[]{:S(2)}) %collective-permute-start.3) | collective-permute-done | bytes 36896 | tf_op jit(solution)/shard_map/ppermute | solution.py:21
  16.4 1.1 %project.1 = (f32[4,4,1536]{2,1,0:T(4,128)S(1)}, bf16[4,4,1536]{2,1,0:T(4,128)(2,1)S(1)}) custom-call(f32[16,1024]{1,0:T(8,128)S(1)} %get-tuple-element.29.kept_ref, f32[16,128]{1,0:T(8,128)S(1)} %get-tuple-element.30.kept_lse_ref, bf16[16,1152]{1,0:T(8,128)(2,1)S(1)} %collective-permute-done.3.got_ref, bf16[2,1024,1536]{2,1,0:T(8,128)(2,1)S(1)} %get-tuple-element.32.w_out_ref), custom_call_target="tpu_custom_call" | custom-call | tf_op jit(solution)/shard_map/project/pallas_call | solution.py:425
  17.5 0.0 collective-permute-start.4
  17.5 1.2 %collective-permute-done.4 = bf16[4,4,1536]{2,1,0:T(4,128)(2,1)S(1)} collective-permute-done((bf16[4,4,1536]{2,1,0:T(4,128)(2,1)S(1)}, bf16[4,4,1536]{2,1,0:T(4,128)(2,1)S(1)}, u32[]{:S(2)}, u32[]{:S(2)}) %collective-permute-start.4) | collective-permute-done | bytes 49184 | tf_op jit(solution)/shard_map/ppermute | solution.py:31
  18.7 0.6 %add_convert_fusion = bf16[4,4,1536]{2,1,0:T(4,128)(2,1)} fusion(f32[4,4,1536]{2,1,0:T(4,128)S(1)} %get-tuple-element.33, bf16[4,4,1536]{2,1,0:T(4,128)(2,1)S(1)} %collective-permute-done.4), kind=kLoop, calls=%fused_computation | loop fusion | flops 73728 | bytes 196608 | tf_op jit(solution)/shard_map/convert_element_type | solution.py:437
Async XLA Ops:
  0.0 7.7 %collective-permute-start = (bf16[4,4,1536]{2,1,0:T(4,128)(2,1)}, bf16[4,4,1536]{2,1,0:T(4,128)(2,1)S(1)}, u32[]{:S(2)}, u32[]{:S(2)}) collective-permute-start(bf16[4,4,1536]{2,1,0:T(4,128)(2,1)} %hidden.1), channel_id=1, source_target_pairs={{0,1},{1,0},{2,3},{3,2},{4,5},{5,4},{6,7},{7,6},{8,9},{9,8},{10,11... | collective-permute-start | bytes 147464 | tf_op jit(solution)/shard_map/ppermute | solution.py:31
  0.5 7.3 %collective-permute-start.2 = (bf16[4,4,1536]{2,1,0:T(4,128)(2,1)}, bf16[4,4,1536]{2,1,0:T(4,128)(2,1)S(1)}, u32[]{:S(2)}, u32[]{:S(2)}) collective-permute-start(bf16[4,4,1536]{2,1,0:T(4,128)(2,1)} %hidden.1), channel_id=1, source_target_pairs={{0,3},{1,2},{2,1},{3,0},{4,7},{5,6},{6,5},{7,4},{8,11},{9,10},{10,... | collective-permute-start | bytes 147464 | tf_op jit(solution)/shard_map/ppermute | solution.py:31
  3.1 4.7 %collective-permute-start.1 = (bf16[4,4,1536]{2,1,0:T(4,128)(2,1)}, bf16[4,4,1536]{2,1,0:T(4,128)(2,1)S(1)}, u32[]{:S(2)}, u32[]{:S(2)}) collective-permute-start(bf16[4,4,1536]{2,1,0:T(4,128)(2,1)} %hidden.1), channel_id=1, source_target_pairs={{0,2},{1,3},{2,0},{3,1},{4,6},{5,7},{6,4},{7,5},{8,10},{9,11},{10,... | collective-permute-start | bytes 147464 | tf_op jit(solution)/shard_map/ppermute | solution.py:31
  12.4 4.0 %collective-permute-start.3 = (bf16[16,1152]{1,0:T(8,128)(2,1)S(1)}, bf16[16,1152]{1,0:T(8,128)(2,1)S(1)}, u32[]{:S(2)}, u32[]{:S(2)}) collective-permute-start(bf16[16,1152]{1,0:T(8,128)(2,1)S(1)} %get-tuple-element.31), channel_id=1, source_target_pairs={{0,2},{2,0},{4,6},{6,4},{8,10},{10,8},{12,14},{14,12},{16,18},{18,... | collective-permute-start | bytes 110600 | tf_op jit(solution)/shard_map/ppermute | solution.py:21
  17.5 1.2 %collective-permute-start.4 = (bf16[4,4,1536]{2,1,0:T(4,128)(2,1)S(1)}, bf16[4,4,1536]{2,1,0:T(4,128)(2,1)S(1)}, u32[]{:S(2)}, u32[]{:S(2)}) collective-permute-start(bf16[4,4,1536]{2,1,0:T(4,128)(2,1)S(1)} %get-tuple-element.34), channel_id=1, source_target_pairs={{0,1},{1,0},{2,3},{3,2},{4,5},{5,4},{6,7},{7,6},{8,9},{9,8},{10,11... | collective-permute-start | bytes 147464 | tf_op jit(solution)/shard_map/ppermute | solution.py:31

commit v4 on v3

--- a/solution.py
+++ b/solution.py
@@ -14,6 +14,14 @@
 norm_eps = 1e-05
 masked_score = -1e30
 rope_base = 500000.0
+
+
+def quotient(x, size):
+    return x >> (size.bit_length() - 1) if size & (size - 1) == 0 else x // size
+
+
+def remainder(x, size):
+    return x & (size - 1) if size & (size - 1) == 0 else x % size
 
 
 def permute_by(value, axis, distance):
@@ -72,24 +80,20 @@
         (hidden, hidden_s),
     ]
     large = []
-    for g in range(kv):
-        cols = pl.ds(g * HD, HD)
-        for prompt, gen, target in ((pk, gk, keys_ref), (pv, gv, values_ref)):
-            large.append((prompt.at[:, :, cols], target.at[g, pl.ds(0, blocks), :, pl.ds(0, HD)]))
-            large.append((gen.at[:, :, cols], target.at[g, pl.ds(blocks, own), :, pl.ds(0, HD)]))
-    for source, target, parts in ((wk, wk_ref, 4), (wq, wq_ref, 8)):
+    for prompt, gen, target in ((pk, gk, keys_ref), (pv, gv, values_ref)):
+        large.append((prompt, target.at[pl.ds(0, blocks)]))
+        large.append((gen, target.at[pl.ds(blocks, own)]))
+    for source, target, parts in ((wk, wk_ref, 4), (wq, wq_ref, 4)):
         size = source.shape[0] // parts
         for n in range(parts):
             place = pl.ds(n * size, size)
-            large.append((source.at[place], target.at[place]))
+            large.append((source.at[place, pl.ds(0, target.shape[1])], target.at[place]))
     copies = [
         pltpu.make_async_copy(source, target, sems.at[n])
         for n, (source, target) in enumerate(small + large)
     ]
     for copy in copies:
         copy.start()
-    for g in range(kv):
-        values_ref[g, :, :, pl.ds(HD, HD)] = jnp.ones((blocks + own, history, HD), jnp.bfloat16)
     for copy in copies[: len(small)]:
         copy.wait()
 
@@ -100,8 +104,8 @@
     row = lax.broadcasted_iota(jnp.int32, (2 * rows, HD), 0)
     lane = lax.broadcasted_iota(jnp.int32, (2 * rows, HD), 1)
     half_dim = HD // 2
-    inverse = jnp.exp((lane % half_dim).astype(jnp.float32) * (-math.log(rope_base) / half_dim))
-    step = (row % rows) // own
+    inverse = jnp.exp(remainder(lane, half_dim).astype(jnp.float32) * (-math.log(rope_base) / half_dim))
+    step = quotient(remainder(row, rows), own)
     angle = (length + history + step).astype(jnp.float32) * inverse
     sine = jnp.sin(angle)
     cosine_ref[...] = jnp.cos(angle)
@@ -115,10 +119,10 @@
             out = jnp.where(beam == j, parents_s[s, request * BEAMS + j], out)
         return out
 
-    row = lax.broadcasted_iota(jnp.int32, (count, HD), 0) % (2 * rows)
-    row_step = (row % rows) // own
+    row = remainder(lax.broadcasted_iota(jnp.int32, (count, HD), 0), 2 * rows)
+    row_step = quotient(remainder(row, rows), own)
     row_parity = jnp.where(row < rows, parity, 1 - parity)
-    beam = row_parity * own + row % own
+    beam = row_parity * own + remainder(row, own)
     ancestors = [None] * steps
     at = beam
     for s in reversed(range(steps)):
@@ -132,13 +136,15 @@
         place = parity * half_len + c * HD + lane
         bias_ref[:, pl.ds(c * HD, HD)] = jnp.where(place < length, 0.0, masked_score)
     for c in range(own * history // HD):
-        key_beam = parity * own + (c * HD + lane) // history
+        key_beam = parity * own + quotient(c * HD + lane, history)
         bias_ref[:, pl.ds(half_len + c * HD, HD)] = jnp.where(
             key_beam == origin, 0.0, masked_score
         )
     new_bias = jnp.full((count, HD), masked_score, jnp.float32)
     for s in range(steps):
-        hit = (lane // own == s) & (ancestors[s] == parity * own + lane % own)
+        hit = (quotient(lane, own) == s) & (
+            ancestors[s] == parity * own + remainder(lane, own)
+        )
         new_bias = jnp.where(hit, 0.0, new_bias)
     bias_ref[:, pl.ds(half_len + own * history, HD)] = new_bias
     for copy in copies[len(small) :]:
@@ -156,28 +162,26 @@
     cosine_ref,
     sine_ref,
     bias_ref,
+    wq,
     wv,
-    w_out,
     *refs,
 ):
     steps, own, tp, kv, group = sizes
     pieces = (None,) + refs[: 2 * tp - 1]
-    kept_ref, kept_lse_ref, sent_ref, w_out_ref, x_s, xn_s, wv_s, sems = refs[2 * tp - 1 :]
+    kept_ref, kept_lse_ref, sent_ref, x_s, xn_s, wq_s, wv_s, sems = refs[2 * tp - 1 :]
     rows = steps * own
     part = x_ref.shape[-1]
     width = part * tp
     heads = kv * group
-    old = keys_ref.shape[1] * keys_ref.shape[2]
+    old = keys_ref.shape[0] * keys_ref.shape[1]
     me_tp = lax.axis_index("tp")
 
-    copies = [pltpu.make_async_copy(wv, wv_s, sems.at[tp])]
-    copies += [
-        pltpu.make_async_copy(
-            w_out.at[:, pl.ds(pl.multiple_of((me_tp ^ d) * part, HD), part)],
-            w_out_ref.at[d],
-            sems.at[d],
-        )
-        for d in range(tp)
+    near = wq_ref.shape[1]
+    halves = [(wq.at[:, pl.ds(near, wq_s.shape[1])], wq_s)] if near < wq.shape[1] else []
+    halves.append((wv, wv_s))
+    copies = [
+        pltpu.make_async_copy(source, target, sems.at[n])
+        for n, (source, target) in enumerate(halves)
     ]
     for copy in copies:
         copy.start()
@@ -221,17 +225,25 @@
 
     pad = jnp.zeros((HD - rows, HD), jnp.bfloat16)
     ones = jnp.ones((HD, HD), jnp.bfloat16)
+    old_ones = jnp.ones((old, HD), jnp.bfloat16)
     contract = (((1,), (1,)), ((), ()))
     new_keys = [
         jnp.concatenate([rotate(x, key_tables)[:rows], pad], axis=0) for x in project_all(wk_ref)
     ]
 
     def score(g):
+        lower = g * group * HD
+        if lower == near:
+            copies[0].wait()
+        source, lower = (wq_ref, lower) if lower < near else (wq_s, lower - near)
         q = jnp.concatenate(
-            [rotate(x, query_tables) for x in project(wq_ref, g * group * HD, group * HD)], axis=0
+            [rotate(x, query_tables) for x in project(source, lower, group * HD)], axis=0
         )
         before = lax.dot_general(
-            q, keys_ref[g].reshape(old, HD), contract, preferred_element_type=jnp.float32
+            q,
+            keys_ref[:, :, pl.ds(g * HD, HD)].reshape(old, HD),
+            contract,
+            preferred_element_type=jnp.float32,
         )
         now = lax.dot_general(q, new_keys[g], contract, preferred_element_type=jnp.float32)
         return before + bias_ref[:, pl.ds(0, old)], now + bias_ref[:, pl.ds(old, HD)]
@@ -254,7 +266,7 @@
             soft.append(soften(*scores[g - 1]))
     soft.append(soften(*scores[kv - 1]))
 
-    copies[0].wait()
+    copies[-1].wait()
     new_values = [
         jnp.concatenate([(x * scale).astype(jnp.bfloat16)[:rows], pad], axis=0)
         for x in project_all(wv_s)
@@ -264,8 +276,11 @@
     sent_lse = jnp.zeros((rows, HD), jnp.float32)
     for g in range(kv):
         before, now, top = soft[g]
+        old_values = values_ref[:, :, pl.ds(g * HD, HD)].reshape(old, HD)
         mixed = jnp.dot(
-            before, values_ref[g].reshape(old, 2 * HD), preferred_element_type=jnp.float32
+            before,
+            jnp.concatenate([old_values, old_ones], axis=1),
+            preferred_element_type=jnp.float32,
         ) + jnp.dot(
             now,
             jnp.concatenate([new_values[g], ones], axis=1),
@@ -291,14 +306,13 @@
         terms = jnp.where(lane // heads == n, term, terms)
         rest = rest - term
     sent_ref[:, pl.ds(heads * HD, HD)] = terms.astype(jnp.bfloat16)
-    for copy in copies[1:]:
-        copy.wait()
 
 
 def project_kernel(sizes, kept_ref, kept_lse_ref, got_ref, w_out_ref, *refs):
     steps, own, tp, heads, chunk = sizes
     outs = refs[:tp]
     (ctx_s,) = refs[tp:]
+    me_tp = lax.axis_index("tp")
     part = outs[0].shape[-1]
     base = heads * HD
     lse_mine = kept_lse_ref[...]
@@ -317,7 +331,8 @@
     for d in list(range(1, tp)) + [0]:
         for lower in range(0, part, chunk):
             cols = pl.ds(lower, chunk)
-            out = jnp.dot(ctx_s[...], w_out_ref[d, :, cols], preferred_element_type=jnp.float32)
+            place = pl.ds(pl.multiple_of((me_tp ^ d) * part + lower, HD), chunk)
+            out = jnp.dot(ctx_s[...], w_out_ref[:, place], preferred_element_type=jnp.float32)
             for s in range(steps):
                 outs[d][s, :, cols] = out[s * own : (s + 1) * own].astype(outs[d].dtype)
 
@@ -357,16 +372,17 @@
     params = pltpu.CompilerParams(vmem_limit_bytes=16 * 2**20)
     f32, bf16 = jnp.float32, jnp.bfloat16
     blocks = prompt_keys.shape[1] // history
-    old = (kv, blocks + own, history)
+    old = (blocks + own, history, kv * HD)
+    near = max(kv // 2, 1) * group * HD
     loaded = pl.pallas_call(
         functools.partial(load_kernel, (steps, own, kv, group, history)),
         out_shape=(
             jax.ShapeDtypeStruct((1, width), f32),
             jax.ShapeDtypeStruct((rows, part), f32),
-            jax.ShapeDtypeStruct(w_query.shape, bf16),
+            jax.ShapeDtypeStruct((width, near), bf16),
             jax.ShapeDtypeStruct(w_key.shape, bf16),
-            jax.ShapeDtypeStruct((*old, HD), bf16),
-            jax.ShapeDtypeStruct((*old, 2 * HD), bf16),
+            jax.ShapeDtypeStruct(old, bf16),
+            jax.ShapeDtypeStruct(old, bf16),
             jax.ShapeDtypeStruct((2 * rows, HD), f32),
             jax.ShapeDtypeStruct((2 * rows, HD), f32),
             jax.ShapeDtypeStruct((group * 2 * rows, (blocks + own) * history + HD), f32),
@@ -377,7 +393,7 @@
             pltpu.SMEM(lengths.shape, jnp.int32),
             pltpu.SMEM(parents.shape, jnp.int32),
             pltpu.VMEM(hidden_in.shape, bf16),
-            pltpu.SemaphoreType.DMA((16 + 4 * kv,)),
+            pltpu.SemaphoreType.DMA((16,)),
         ],
         compiler_params=params,
         name="load",
@@ -399,25 +415,25 @@
         )
     )
 
-    kept, kept_lse, sent, w_out_near = pl.pallas_call(
+    kept, kept_lse, sent = pl.pallas_call(
         functools.partial(attend_kernel, (steps, own, tp, kv, group)),
         out_shape=(
             jax.ShapeDtypeStruct((rows, heads * HD), f32),
             jax.ShapeDtypeStruct((rows, HD), f32),
             jax.ShapeDtypeStruct((rows, heads * HD + HD), bf16),
-            jax.ShapeDtypeStruct((tp, heads * HD, part), bf16),
         ),
         in_specs=[vmem] * 9 + [hbm] * 2 + [vmem] * (2 * tp - 1),
-        out_specs=(vmem,) * 4,
+        out_specs=(vmem,) * 3,
         scratch_shapes=[
             pltpu.VMEM((2 * tp, rows, part), f32),
             pltpu.VMEM((2 * rows, width), bf16),
+            pltpu.VMEM((width, near), bf16),
             pltpu.VMEM(w_value.shape, bf16),
-            pltpu.SemaphoreType.DMA((tp + 1,)),
+            pltpu.SemaphoreType.DMA((2,)),
         ],
         compiler_params=params,
         name="attend",
-    )(*loaded, in_hbm(w_value), in_hbm(w_out), *pieces)
+    )(*loaded, in_hbm(w_query), in_hbm(w_value), *pieces)
 
     got = permute_by(sent, "req", 1)
 
@@ -430,7 +446,7 @@
         scratch_shapes=[pltpu.VMEM((rows, heads * HD), bf16)],
         compiler_params=params,
         name="project",
-    )(kept, kept_lse, got, w_out_near)
+    )(kept, kept_lse, got, pltpu.with_memory_space_constraint(w_out, pltpu.VMEM))
     total = sums[0]
     for t in range(1, tp):
         total = total + across(sums[t], 0, t).astype(f32)

time: 19.5 us -> 20 us (1.026)
  waiting for transfers between devices: 3.18 us -> 4.83 us
  starting transfers between devices: 5.14 us -> 4.34 us
  Pallas kernels: 10.4 us -> 10 us
    pallas_call x1, Pallas kernels: 4.64 us -> 3.42 us  [body(): pl.pallas_call(functools.partial(load_kernel, (steps, own, kv, group, his...]
    pallas_call x1, Pallas kernels: 4.66 us -> 5.51 us  [body(): pl.pallas_call(functools.partial(attend_kernel, (steps, own, tp, kv, grou...]
    ppermute x4, waiting for transfers between devices: 1.24 us -> 2.09 us  [across(): return lax.ppermute(value, ('req', 'tp'), pairs)]
    ppermute x1, waiting for transfers between devices: 1.94 us -> 2.74 us  [permute_by(): return lax.ppermute(value, axis, pairs)]
    ppermute x1, starting transfers between devices: 2.08 us -> 1.28 us  [permute_by(): return lax.ppermute(value, axis, pairs)]
  transfers between devices with their start and end apart: 5 -> 5, of which waited for: 2 -> 3; matrix products, arithmetic and copies ran while one was open for 0% -> 0% of each run, Pallas kernels for 24% -> 17%
where the time goes in v4:
time: 20 us; the launch traced here: 19.9 us
  Pallas kernels  10 us (50%)
  waiting for transfers between devices  4.83 us (24%)
  starting transfers between devices  4.34 us (22%)
  other arithmetic  0.65 us (3%)
    pallas_call x1, Pallas kernels, body(): pl.pallas_call(functools.partial(attend_kernel, (steps, own, tp, kv, grou...  5.51 us
    pallas_call x1, Pallas kernels, body(): pl.pallas_call(functools.partial(load_kernel, (steps, own, kv, group, his...  3.42 us
    ppermute x4, starting transfers between devices, across(): return lax.ppermute(value, ('req', 'tp'), pairs)  3.06 us
    ppermute x1, waiting for transfers between devices, permute_by(): return lax.ppermute(value, axis, pairs)  2.74 us
    ppermute x4, waiting for transfers between devices, across(): return lax.ppermute(value, ('req', 'tp'), pairs)  2.09 us
    ppermute x1, starting transfers between devices, permute_by(): return lax.ppermute(value, axis, pairs)  1.28 us
    pallas_call x1, Pallas kernels, body(): pl.pallas_call(functools.partial(project_kernel, (steps, own, tp, heads,...  1.08 us
    convert_element_type x1, other arithmetic, body(): return total.astype(bf16)  0.65 us
  transfers between devices with their start and end apart: 5, of which 3 were waited for; matrix products, arithmetic and copies ran while one was open for 0% of the time, Pallas kernels for 17%

profile of v4, /device:TPU:0, one launch (start us, length us, event | category | flops | bytes accessed | tf_op | source)
XLA Modules:
  0.0 19.9 jit_solution(8699759964381165872)
XLA Ops:
  0.0 0.5 %collective-permute-start = (bf16[4,4,1536]{2,1,0:T(4,128)(2,1)}, bf16[4,4,1536]{2,1,0:T(4,128)(2,1)S(1)}, u32[]{:S(2)}, u32[]{:S(2)}) collective-permute-start(bf16[4,4,1536]{2,1,0:T(4,128)(2,1)} %hidden.1), channel_id=1, source_target_pairs={{0,1},{1,0},{2,3},{3,2},{4,5},{5,4},{6,7},{7,6},{8,9},{9,8},{10,11... | collective-permute-start | bytes 147464 | tf_op jit(solution)/shard_map/ppermute | solution.py:39
  0.5 2.6 %collective-permute-start.2 = (bf16[4,4,1536]{2,1,0:T(4,128)(2,1)}, bf16[4,4,1536]{2,1,0:T(4,128)(2,1)S(1)}, u32[]{:S(2)}, u32[]{:S(2)}) collective-permute-start(bf16[4,4,1536]{2,1,0:T(4,128)(2,1)} %hidden.1), channel_id=1, source_target_pairs={{0,3},{1,2},{2,1},{3,0},{4,7},{5,6},{6,5},{7,4},{8,11},{9,10},{10,... | collective-permute-start | bytes 147464 | tf_op jit(solution)/shard_map/ppermute | solution.py:39
  3.1 0.0 collective-permute-start.1
  3.1 3.4 %load.1 = (f32[1,3072]{1,0:T(1,128)S(1)}, f32[16,1536]{1,0:T(8,128)S(1)}, bf16[3072,512]{1,0:T(8,128)(2,1)S(1)}, bf16[3072,512]{1,0:T(8,128)(2,1)S(1)}, bf16[12,...) custom-call(s32[8]{0:T(128)} %lengths.1, ...), custom_call_target="tpu_custom_call" | custom-call | tf_op jit(solution)/shard_map/load/pallas_call | solution.py:377
  6.5 0.0 collective-permute-done.refs_0_
  6.5 0.0 collective-permute-done.2.refs_2_
  6.5 0.8 %collective-permute-done.1.refs_1_ = bf16[4,4,1536]{2,1,0:T(4,128)(2,1)S(1)} collective-permute-done((bf16[4,4,1536]{2,1,0:T(4,128)(2,1)}, bf16[4,4,1536]{2,1,0:T(4,128)(2,1)S(1)}, u32[]{:S(2)}, u32[]{:S(2)}) %collective-permute-start.1) | collective-permute-done | bytes 49184 | tf_op jit(solution)/shard_map/ppermute | solution.py:39
  7.4 0.0 slice-start
  7.4 0.0 slice-start.1
  7.4 5.5 %attend.1 = (f32[16,1024]{1,0:T(8,128)S(1)}, f32[16,128]{1,0:T(8,128)S(1)}, bf16[16,1152]{1,0:T(8,128)(2,1)S(1)}) custom-call(f32[1,3072]{1,0:T(1,128)S(1)} %get-tuple-element.19.gain_ref, f32[16,1536]{1,0:T(8,128)S(1)} %get-tuple-element.20.x_ref, bf16[3072,512]{1,0:T(8,128)(2,1)S(1)} %get-tuple-element.21.wq_ref, ...), custom_call_target="tpu_custom_call" | custom-call | tf_op jit(solution)/shard_map/attend/pallas_call | solution.py:418
  12.9 1.3 %collective-permute-start.3 = (bf16[16,1152]{1,0:T(8,128)(2,1)S(1)}, bf16[16,1152]{1,0:T(8,128)(2,1)S(1)}, u32[]{:S(2)}, u32[]{:S(2)}) collective-permute-start(bf16[16,1152]{1,0:T(8,128)(2,1)S(1)} %get-tuple-element.30), channel_id=1, source_target_pairs={{0,2},{2,0},{4,6},{6,4},{8,10},{10,8},{12,14},{14,12},{16,18},{18,... | collective-permute-start | bytes 110600 | tf_op jit(solution)/shard_map/ppermute | solution.py:29
  14.2 2.7 %collective-permute-done.3.got_ref = bf16[16,1152]{1,0:T(8,128)(2,1)S(1)} collective-permute-done((bf16[16,1152]{1,0:T(8,128)(2,1)S(1)}, bf16[16,1152]{1,0:T(8,128)(2,1)S(1)}, u32[]{:S(2)}, u32[]{:S(2)}) %collective-permute-start.3) | collective-permute-done | bytes 36896 | tf_op jit(solution)/shard_map/ppermute | solution.py:29
  16.9 0.0 slice-done
  16.9 0.0 slice-done.1
  16.9 1.1 %project.1 = (f32[4,4,1536]{2,1,0:T(4,128)S(1)}, bf16[4,4,1536]{2,1,0:T(4,128)(2,1)S(1)}) custom-call(f32[16,1024]{1,0:T(8,128)S(1)} %get-tuple-element.28.kept_ref, f32[16,128]{1,0:T(8,128)S(1)} %get-tuple-element.29.kept_lse_ref, bf16[16,1152]{1,0:T(8,128)(2,1)S(1)} %collective-permute-done.3.got_ref, bf16[1024,3072]{1,0:T(8,128)(2,1)S(1)} %bitcast.4), custom_call_target="tpu_custom_call" | custom-call | tf_op jit(solution)/shard_map/project/pallas_call | solution.py:441
  18.0 0.0 collective-permute-start.4
  18.0 1.2 %collective-permute-done.4 = bf16[4,4,1536]{2,1,0:T(4,128)(2,1)S(1)} collective-permute-done((bf16[4,4,1536]{2,1,0:T(4,128)(2,1)S(1)}, bf16[4,4,1536]{2,1,0:T(4,128)(2,1)S(1)}, u32[]{:S(2)}, u32[]{:S(2)}) %collective-permute-start.4) | collective-permute-done | bytes 49184 | tf_op jit(solution)/shard_map/ppermute | solution.py:39
  19.2 0.6 %add_convert_fusion = bf16[4,4,1536]{2,1,0:T(4,128)(2,1)} fusion(f32[4,4,1536]{2,1,0:T(4,128)S(1)} %get-tuple-element.31, bf16[4,4,1536]{2,1,0:T(4,128)(2,1)S(1)} %collective-permute-done.4), kind=kLoop, calls=%fused_computation | loop fusion | flops 73728 | bytes 196608 | tf_op jit(solution)/shard_map/convert_element_type | solution.py:453
  (1 shorter events, 0.0 us)
Async XLA Ops:
  0.0 6.5 %collective-permute-start = (bf16[4,4,1536]{2,1,0:T(4,128)(2,1)}, bf16[4,4,1536]{2,1,0:T(4,128)(2,1)S(1)}, u32[]{:S(2)}, u32[]{:S(2)}) collective-permute-start(bf16[4,4,1536]{2,1,0:T(4,128)(2,1)} %hidden.1), channel_id=1, source_target_pairs={{0,1},{1,0},{2,3},{3,2},{4,5},{5,4},{6,7},{7,6},{8,9},{9,8},{10,11... | collective-permute-start | bytes 147464 | tf_op jit(solution)/shard_map/ppermute | solution.py:39
  0.5 6.0 %collective-permute-start.2 = (bf16[4,4,1536]{2,1,0:T(4,128)(2,1)}, bf16[4,4,1536]{2,1,0:T(4,128)(2,1)S(1)}, u32[]{:S(2)}, u32[]{:S(2)}) collective-permute-start(bf16[4,4,1536]{2,1,0:T(4,128)(2,1)} %hidden.1), channel_id=1, source_target_pairs={{0,3},{1,2},{2,1},{3,0},{4,7},{5,6},{6,5},{7,4},{8,11},{9,10},{10,... | collective-permute-start | bytes 147464 | tf_op jit(solution)/shard_map/ppermute | solution.py:39
  3.1 4.3 %collective-permute-start.1 = (bf16[4,4,1536]{2,1,0:T(4,128)(2,1)}, bf16[4,4,1536]{2,1,0:T(4,128)(2,1)S(1)}, u32[]{:S(2)}, u32[]{:S(2)}) collective-permute-start(bf16[4,4,1536]{2,1,0:T(4,128)(2,1)} %hidden.1), channel_id=1, source_target_pairs={{0,2},{1,3},{2,0},{3,1},{4,6},{5,7},{6,4},{7,5},{8,10},{9,11},{10,... | collective-permute-start | bytes 147464 | tf_op jit(solution)/shard_map/ppermute | solution.py:39
  7.4 9.6 %slice-start = ((s8[6291456]{0:T(1024)(128)(4,1)}), s8[4194304]{0:T(1024)(128)(4,1)S(1)}, s32[]{:S(2)}) async-start(s8[6291456]{0:T(1024)(128)(4,1)} %bitcast.3), calls=%async_computation | async-start | bytes 8388608
  7.4 9.6 %slice-start.1 = ((s8[6291456]{0:T(1024)(128)(4,1)}), s8[2097152]{0:T(1024)(128)(4,1)S(1)}, s32[]{:S(2)}) async-start(s8[6291456]{0:T(1024)(128)(4,1)} %bitcast.3), calls=%async_computation.1 | async-start | bytes 4194304
  12.9 4.0 %collective-permute-start.3 = (bf16[16,1152]{1,0:T(8,128)(2,1)S(1)}, bf16[16,1152]{1,0:T(8,128)(2,1)S(1)}, u32[]{:S(2)}, u32[]{:S(2)}) collective-permute-start(bf16[16,1152]{1,0:T(8,128)(2,1)S(1)} %get-tuple-element.30), channel_id=1, source_target_pairs={{0,2},{2,0},{4,6},{6,4},{8,10},{10,8},{12,14},{14,12},{16,18},{18,... | collective-permute-start | bytes 110600 | tf_op jit(solution)/shard_map/ppermute | solution.py:29
  18.0 1.2 %collective-permute-start.4 = (bf16[4,4,1536]{2,1,0:T(4,128)(2,1)S(1)}, bf16[4,4,1536]{2,1,0:T(4,128)(2,1)S(1)}, u32[]{:S(2)}, u32[]{:S(2)}) collective-permute-start(bf16[4,4,1536]{2,1,0:T(4,128)(2,1)S(1)} %get-tuple-element.32), channel_id=1, source_target_pairs={{0,1},{1,0},{2,3},{3,2},{4,5},{5,4},{6,7},{7,6},{8,9},{9,8},{10,11... | collective-permute-start | bytes 147464 | tf_op jit(solution)/shard_map/ppermute | solution.py:39

commit v5 on v4

--- a/solution.py
+++ b/solution.py
@@ -308,11 +308,25 @@
     sent_ref[:, pl.ds(heads * HD, HD)] = terms.astype(jnp.bfloat16)
 
 
+def fetch_kernel(kept_lse_ref, w_out, kept_lse_out, w_out_ref, sems):
+    copies = []
+    tp = w_out_ref.shape[0]
+    part = w_out_ref.shape[-1]
+    me_tp = lax.axis_index("tp")
+    for d in range(tp):
+        place = pl.ds(pl.multiple_of((me_tp ^ d) * part, HD), part)
+        copies.append(pltpu.make_async_copy(w_out.at[:, place], w_out_ref.at[d], sems.at[d]))
+    for copy in copies:
+        copy.start()
+    kept_lse_out[...] = kept_lse_ref[...]
+    for copy in copies:
+        copy.wait()
+
+
 def project_kernel(sizes, kept_ref, kept_lse_ref, got_ref, w_out_ref, *refs):
     steps, own, tp, heads, chunk = sizes
     outs = refs[:tp]
     (ctx_s,) = refs[tp:]
-    me_tp = lax.axis_index("tp")
     part = outs[0].shape[-1]
     base = heads * HD
     lse_mine = kept_lse_ref[...]
@@ -331,8 +345,7 @@
     for d in list(range(1, tp)) + [0]:
         for lower in range(0, part, chunk):
             cols = pl.ds(lower, chunk)
-            place = pl.ds(pl.multiple_of((me_tp ^ d) * part + lower, HD), chunk)
-            out = jnp.dot(ctx_s[...], w_out_ref[:, place], preferred_element_type=jnp.float32)
+            out = jnp.dot(ctx_s[...], w_out_ref[d, :, cols], preferred_element_type=jnp.float32)
             for s in range(steps):
                 outs[d][s, :, cols] = out[s * own : (s + 1) * own].astype(outs[d].dtype)
 
@@ -436,6 +449,18 @@
     )(*loaded, in_hbm(w_query), in_hbm(w_value), *pieces)
 
     got = permute_by(sent, "req", 1)
+    kept_lse, w_out_near = pl.pallas_call(
+        fetch_kernel,
+        out_shape=(
+            jax.ShapeDtypeStruct((rows, HD), f32),
+            jax.ShapeDtypeStruct((tp, heads * HD, part), bf16),
+        ),
+        in_specs=[vmem, hbm],
+        out_specs=(vmem, vmem),
+        scratch_shapes=[pltpu.SemaphoreType.DMA((tp,))],
+        compiler_params=params,
+        name="fetch",
+    )(kept_lse, in_hbm(w_out))
 
     out_types = [f32] + [bf16] * (tp - 1)
     sums = pl.pallas_call(
@@ -446,7 +471,7 @@
         scratch_shapes=[pltpu.VMEM((rows, heads * HD), bf16)],
         compiler_params=params,
         name="project",
-    )(kept, kept_lse, got, pltpu.with_memory_space_constraint(w_out, pltpu.VMEM))
+    )(kept, kept_lse, got, w_out_near)
     total = sums[0]
     for t in range(1, tp):
         total = total + across(sums[t], 0, t).astype(f32)

time: 20 us -> 19.4 us (0.970)
  waiting for transfers between devices: 4.83 us -> 2.09 us
  Pallas kernels: 10 us -> 12.1 us
    pallas_call x0 -> x1, Pallas kernels: none -> 2.86 us  [body(): pl.pallas_call(fetch_kernel, out_shape=(jax.ShapeDtypeStruct((rows, HD),...]
    ppermute x1, waiting for transfers between devices: 2.74 us -> 0.01 us  [permute_by(): return lax.ppermute(value, axis, pairs)]
    pallas_call x1, Pallas kernels: 5.51 us -> 4.76 us  [body(): pl.pallas_call(functools.partial(attend_kernel, (steps, own, tp, kv, grou...]
  transfers between devices with their start and end apart: 5 -> 5, of which waited for: 3 -> 2; matrix products, arithmetic and copies ran while one was open for 0% -> 0% of each run, Pallas kernels for 17% -> 33%
where the time goes in v5:
time: 19.4 us; the launch traced here: 19.2 us
  Pallas kernels  12.1 us (62%)
  starting transfers between devices  4.31 us (22%)
  waiting for transfers between devices  2.09 us (11%)
  other arithmetic  0.65 us (3%)
    pallas_call x1, Pallas kernels, body(): pl.pallas_call(functools.partial(attend_kernel, (steps, own, tp, kv, grou...  4.76 us
    pallas_call x1, Pallas kernels, body(): pl.pallas_call(functools.partial(load_kernel, (steps, own, kv, group, his...  3.42 us
    ppermute x4, starting transfers between devices, across(): return lax.ppermute(value, ('req', 'tp'), pairs)  3.06 us
    pallas_call x1, Pallas kernels, body(): pl.pallas_call(fetch_kernel, out_shape=(jax.ShapeDtypeStruct((rows, HD),...  2.86 us
    ppermute x4, waiting for transfers between devices, across(): return lax.ppermute(value, ('req', 'tp'), pairs)  2.09 us
    ppermute x1, starting transfers between devices, permute_by(): return lax.ppermute(value, axis, pairs)  1.25 us
    pallas_call x1, Pallas kernels, body(): pl.pallas_call(functools.partial(project_kernel, (steps, own, tp, heads,...  1.08 us
    convert_element_type x1, other arithmetic, body(): return total.astype(bf16)  0.65 us
  transfers between devices with their start and end apart: 5, of which 2 were waited for; matrix products, arithmetic and copies ran while one was open for 0% of the time, Pallas kernels for 33%

profile of v5, /device:TPU:0, one launch (start us, length us, event | category | flops | bytes accessed | tf_op | source)
XLA Modules:
  0.0 19.2 jit_solution(17391465520088728589)
XLA Ops:
  0.0 0.5 %collective-permute-start = (bf16[4,4,1536]{2,1,0:T(4,128)(2,1)}, bf16[4,4,1536]{2,1,0:T(4,128)(2,1)S(1)}, u32[]{:S(2)}, u32[]{:S(2)}) collective-permute-start(bf16[4,4,1536]{2,1,0:T(4,128)(2,1)} %hidden.1), channel_id=1, source_target_pairs={{0,1},{1,0},{2,3},{3,2},{4,5},{5,4},{6,7},{7,6},{8,9},{9,8},{10,11... | collective-permute-start | bytes 147464 | tf_op jit(solution)/shard_map/ppermute | solution.py:39
  0.5 2.6 %collective-permute-start.2 = (bf16[4,4,1536]{2,1,0:T(4,128)(2,1)}, bf16[4,4,1536]{2,1,0:T(4,128)(2,1)S(1)}, u32[]{:S(2)}, u32[]{:S(2)}) collective-permute-start(bf16[4,4,1536]{2,1,0:T(4,128)(2,1)} %hidden.1), channel_id=1, source_target_pairs={{0,3},{1,2},{2,1},{3,0},{4,7},{5,6},{6,5},{7,4},{8,11},{9,10},{10,... | collective-permute-start | bytes 147464 | tf_op jit(solution)/shard_map/ppermute | solution.py:39
  3.1 0.0 collective-permute-start.1
  3.1 3.4 %load.1 = (f32[1,3072]{1,0:T(1,128)S(1)}, f32[16,1536]{1,0:T(8,128)S(1)}, bf16[3072,512]{1,0:T(8,128)(2,1)S(1)}, bf16[3072,512]{1,0:T(8,128)(2,1)S(1)}, bf16[12,...) custom-call(s32[8]{0:T(128)} %lengths.1, ...), custom_call_target="tpu_custom_call" | custom-call | tf_op jit(solution)/shard_map/load/pallas_call | solution.py:390
  6.5 0.0 collective-permute-done.refs_0_
  6.5 0.0 collective-permute-done.2.refs_2_
  6.5 0.8 %collective-permute-done.1.refs_1_ = bf16[4,4,1536]{2,1,0:T(4,128)(2,1)S(1)} collective-permute-done((bf16[4,4,1536]{2,1,0:T(4,128)(2,1)}, bf16[4,4,1536]{2,1,0:T(4,128)(2,1)S(1)}, u32[]{:S(2)}, u32[]{:S(2)}) %collective-permute-start.1) | collective-permute-done | bytes 49184 | tf_op jit(solution)/shard_map/ppermute | solution.py:39
  7.4 4.8 %attend.1 = (f32[16,1024]{1,0:T(8,128)S(1)}, f32[16,128]{1,0:T(8,128)S(1)}, bf16[16,1152]{1,0:T(8,128)(2,1)S(1)}) custom-call(f32[1,3072]{1,0:T(1,128)S(1)} %get-tuple-element.21.gain_ref, f32[16,1536]{1,0:T(8,128)S(1)} %get-tuple-element.22.x_ref, bf16[3072,512]{1,0:T(8,128)(2,1)S(1)} %get-tuple-element.23.wq_ref, ...), custom_call_target="tpu_custom_call" | custom-call | tf_op jit(solution)/shard_map/attend/pallas_call | solution.py:431
  12.1 1.3 %collective-permute-start.3 = (bf16[16,1152]{1,0:T(8,128)(2,1)S(1)}, bf16[16,1152]{1,0:T(8,128)(2,1)S(1)}, u32[]{:S(2)}, u32[]{:S(2)}) collective-permute-start(bf16[16,1152]{1,0:T(8,128)(2,1)S(1)} %get-tuple-element.33), channel_id=1, source_target_pairs={{0,2},{2,0},{4,6},{6,4},{8,10},{10,8},{12,14},{14,12},{16,18},{18,... | collective-permute-start | bytes 110600 | tf_op jit(solution)/shard_map/ppermute | solution.py:29
  13.4 2.9 %fetch.1 = (f32[16,128]{1,0:T(8,128)S(1)}, bf16[2,1024,1536]{2,1,0:T(8,128)(2,1)S(1)}) custom-call(f32[16,128]{1,0:T(8,128)S(1)} %get-tuple-element.31.kept_lse_ref, bf16[1024,3072]{1,0:T(8,128)(2,1)} %w_out.1), custom_call_target="tpu_custom_call" | custom-call | tf_op jit(solution)/shard_map/fetch/pallas_call | solution.py:452
  16.3 0.0 collective-permute-done.3.got_ref
  16.3 1.1 %project.1 = (f32[4,4,1536]{2,1,0:T(4,128)S(1)}, bf16[4,4,1536]{2,1,0:T(4,128)(2,1)S(1)}) custom-call(f32[16,1024]{1,0:T(8,128)S(1)} %get-tuple-element.30.kept_ref, f32[16,128]{1,0:T(8,128)S(1)} %get-tuple-element.32.kept_lse_ref, bf16[16,1152]{1,0:T(8,128)(2,1)S(1)} %collective-permute-done.3.got_ref, bf16[2,1024,1536]{2,1,0:T(8,128)(2,1)S(1)} %get-tuple-element.34.w_out_ref), custom_call_target="tpu_custom_call" | custom-call | tf_op jit(solution)/shard_map/project/pallas_call | solution.py:466
  17.3 0.0 collective-permute-start.4
  17.3 1.2 %collective-permute-done.4 = bf16[4,4,1536]{2,1,0:T(4,128)(2,1)S(1)} collective-permute-done((bf16[4,4,1536]{2,1,0:T(4,128)(2,1)S(1)}, bf16[4,4,1536]{2,1,0:T(4,128)(2,1)S(1)}, u32[]{:S(2)}, u32[]{:S(2)}) %collective-permute-start.4) | collective-permute-done | bytes 49184 | tf_op jit(solution)/shard_map/ppermute | solution.py:39
  18.6 0.7 %add_convert_fusion = bf16[4,4,1536]{2,1,0:T(4,128)(2,1)} fusion(f32[4,4,1536]{2,1,0:T(4,128)S(1)} %get-tuple-element.35, bf16[4,4,1536]{2,1,0:T(4,128)(2,1)S(1)} %collective-permute-done.4), kind=kLoop, calls=%fused_computation | loop fusion | flops 73728 | bytes 196608 | tf_op jit(solution)/shard_map/convert_element_type | solution.py:478
Async XLA Ops:
  0.0 6.5 %collective-permute-start = (bf16[4,4,1536]{2,1,0:T(4,128)(2,1)}, bf16[4,4,1536]{2,1,0:T(4,128)(2,1)S(1)}, u32[]{:S(2)}, u32[]{:S(2)}) collective-permute-start(bf16[4,4,1536]{2,1,0:T(4,128)(2,1)} %hidden.1), channel_id=1, source_target_pairs={{0,1},{1,0},{2,3},{3,2},{4,5},{5,4},{6,7},{7,6},{8,9},{9,8},{10,11... | collective-permute-start | bytes 147464 | tf_op jit(solution)/shard_map/ppermute | solution.py:39
  0.5 6.0 %collective-permute-start.2 = (bf16[4,4,1536]{2,1,0:T(4,128)(2,1)}, bf16[4,4,1536]{2,1,0:T(4,128)(2,1)S(1)}, u32[]{:S(2)}, u32[]{:S(2)}) collective-permute-start(bf16[4,4,1536]{2,1,0:T(4,128)(2,1)} %hidden.1), channel_id=1, source_target_pairs={{0,3},{1,2},{2,1},{3,0},{4,7},{5,6},{6,5},{7,4},{8,11},{9,10},{10,... | collective-permute-start | bytes 147464 | tf_op jit(solution)/shard_map/ppermute | solution.py:39
  3.1 4.3 %collective-permute-start.1 = (bf16[4,4,1536]{2,1,0:T(4,128)(2,1)}, bf16[4,4,1536]{2,1,0:T(4,128)(2,1)S(1)}, u32[]{:S(2)}, u32[]{:S(2)}) collective-permute-start(bf16[4,4,1536]{2,1,0:T(4,128)(2,1)} %hidden.1), channel_id=1, source_target_pairs={{0,2},{1,3},{2,0},{3,1},{4,6},{5,7},{6,4},{7,5},{8,10},{9,11},{10,... | collective-permute-start | bytes 147464 | tf_op jit(solution)/shard_map/ppermute | solution.py:39
  12.1 4.1 %collective-permute-start.3 = (bf16[16,1152]{1,0:T(8,128)(2,1)S(1)}, bf16[16,1152]{1,0:T(8,128)(2,1)S(1)}, u32[]{:S(2)}, u32[]{:S(2)}) collective-permute-start(bf16[16,1152]{1,0:T(8,128)(2,1)S(1)} %get-tuple-element.33), channel_id=1, source_target_pairs={{0,2},{2,0},{4,6},{6,4},{8,10},{10,8},{12,14},{14,12},{16,18},{18,... | collective-permute-start | bytes 110600 | tf_op jit(solution)/shard_map/ppermute | solution.py:29
  17.3 1.2 %collective-permute-start.4 = (bf16[4,4,1536]{2,1,0:T(4,128)(2,1)S(1)}, bf16[4,4,1536]{2,1,0:T(4,128)(2,1)S(1)}, u32[]{:S(2)}, u32[]{:S(2)}) collective-permute-start(bf16[4,4,1536]{2,1,0:T(4,128)(2,1)S(1)} %get-tuple-element.36), channel_id=1, source_target_pairs={{0,1},{1,0},{2,3},{3,2},{4,5},{5,4},{6,7},{7,6},{8,9},{9,8},{10,11... | collective-permute-start | bytes 147464 | tf_op jit(solution)/shard_map/ppermute | solution.py:39
